TPU v7x, 32 devices: a whole 2x2x4 slice. The times are simulated.
32 devices in a mesh: vec: 4 (over y, core), lat: 2 (over x), lon: 4 (over z).
Axes of the slice: x: 2, y: 2, z: 4, core: 2. Of those that a mesh axis runs over, the one named last changes fastest.
Arguments:
- basis: bfloat16 [4, 5, 48, 16, 512], P('vec', None, None, 'lat', 'lon'), may hold values from -4 to 4
- trajectory: bfloat16 [4, 5, 48, 16, 512], P('vec', None, None, 'lat', 'lon'), may hold values from -4 to 4
- slice_owner: int32 [4], replicated, may hold values from 0 to 3, each once
- diffusion: float32 [5, 47], replicated, may hold values from 0.05 to 2
- energy_weight: float32 [5], replicated, may hold values from 0.5 to 2
Outputs:
- residual_block: float32 [4, 5, 48, 16, 512], P('vec', None, None, 'lat', 'lon')
- coupling: float32 [4, 4], replicated
Inputs may be any that keep to these rules, and one draw needn't show every extreme that they name: `slice_owner`: a permutation: each vector group holds the slice of exactly one timestep.
All inputs are finite; a program needn't handle non-finite values.
Results may differ from a plain program's by a relative error of at most 0.0024.
Values may be sent and summed in bfloat16 or wider, within the bound.
A program may use at most 64 MiB of HBM per device.

v0:
```python
import jax
import jax.numpy as jnp
from jax import lax
from jax.sharding import PartitionSpec as P

STEPS = 2


COURANT = 0.25
HIGH = lax.Precision.HIGHEST


def broadcast(block, axis, holder):
    block = jnp.where(lax.axis_index(axis) == holder, block, jnp.zeros_like(block))
    return lax.psum(block, axis)


def with_halo(block, sides, width, periodic):
    for axis, dim in sides:
        count = lax.axis_size(axis)
        forward = [(i, i + 1) for i in range(count - 1)]
        if periodic:
            forward.append((count - 1, 0))
        backward = [(target, source) for source, target in forward]
        low = lax.ppermute(
            lax.slice_in_dim(block, block.shape[dim] - width, None, axis=dim), axis, forward
        )
        high = lax.ppermute(lax.slice_in_dim(block, 0, width, axis=dim), axis, backward)
        block = jnp.concatenate([low, block, high], axis=dim)
    return block


def implicit_inverse(diffusion):
    level_count = diffusion.shape[1] + 1
    below_k = jnp.pad(diffusion, ((0, 0), (0, 1)))
    above_k = jnp.pad(diffusion, ((0, 0), (1, 0)))
    levels = jnp.arange(level_count)
    above_diag = (levels[:, None] + 1 == levels[None, :]).astype(jnp.float32)[None] * below_k[
        :, :, None
    ]
    identity_mat = jnp.eye(level_count, dtype=jnp.float32)
    matrix = (
        identity_mat[None] * (1.0 + below_k + above_k)[:, :, None]
        - above_diag
        - jnp.swapaxes(above_diag, 1, 2)
    )
    factor = jnp.linalg.cholesky(matrix)
    inverse_factor = lax.linalg.triangular_solve(
        factor, jnp.broadcast_to(identity_mat, matrix.shape), left_side=True, lower=True
    )
    return jnp.einsum("fkl,fkm->flm", inverse_factor, inverse_factor, precision=HIGH)


def tendency(field, field_lat, field_lon, state, state_lat, state_lon):
    field_dlon = (field_lon[..., 2:] - field_lon[..., :-2]) * 0.5
    field_dlat = (field_lat[..., 2:, :] - field_lat[..., :-2, :]) * 0.5
    state_dlon = (state_lon[..., 2:] - state_lon[..., :-2]) * 0.5
    state_dlat = (state_lat[..., 2:, :] - state_lat[..., :-2, :]) * 0.5
    wind_u = state[0]
    wind_v = state[1]
    return (
        wind_u * field_dlon
        + wind_v * field_dlat
        + field[:, 0:1] * state_dlon
        + field[:, 1:2] * state_dlat
    )


def per_device(basis, trajectory, slice_owner, diffusion, energy_weight):
    inverse = implicit_inverse(diffusion)
    field = basis.astype(jnp.float32)
    lat_index = lax.axis_index("lat")
    lat_count = lax.axis_size("lat")
    rows = basis.shape[3]
    columns_dev = basis.shape[4]
    for timestep in range(STEPS):
        root = slice_owner[timestep]
        state = broadcast(trajectory[0], "vec", root)
        state_lat = with_halo(state, (("lat", 2),), 1, False)
        state_lon = with_halo(state, (("lon", 3),), 1, True)
        field_lat = with_halo(field.astype(jnp.bfloat16), (("lat", 3),), 1, False).astype(
            field.dtype
        )
        field_lon = with_halo(field.astype(jnp.bfloat16), (("lon", 4),), 1, True).astype(
            field.dtype
        )
        change = tendency(
            field,
            field_lat,
            field_lon,
            state.astype(jnp.float32),
            state_lat.astype(jnp.float32),
            state_lon.astype(jnp.float32),
        )
        moved = field - COURANT * change
        field = jnp.einsum("fkl,vflyx->vfkyx", inverse, moved, precision=HIGH)
    all_basis = lax.all_gather(basis, "vec", axis=0, tiled=True)
    total_rows = rows * lat_count
    row_ids = (lat_index * rows + jnp.arange(rows)).astype(jnp.float32)
    latitude = (row_ids + 0.5) * (jnp.pi / total_rows) - jnp.pi / 2
    total = float(basis.shape[1] * basis.shape[2] * total_rows * columns_dev * lax.axis_size("lon"))
    scale = energy_weight[:, None, None, None] * jnp.cos(latitude)[None, None, :, None] / total
    weighted = field * scale
    partial_gram = jnp.einsum(
        "iflyx,jflyx->ij", all_basis, weighted, precision=HIGH, preferred_element_type=jnp.float32
    )
    own_columns = lax.psum(partial_gram, ("lat", "lon"))
    coupling = lax.all_gather(own_columns, "vec", axis=1, tiled=True)
    residual_block = field - jnp.einsum(
        "iflyx,ij->jflyx",
        all_basis,
        own_columns,
        precision=HIGH,
        preferred_element_type=jnp.float32,
    )
    return (residual_block, coupling)


def solution(mesh):
    return jax.shard_map(
        per_device,
        mesh=mesh,
        in_specs=(
            P("vec", None, None, "lat", "lon"),
            P("vec", None, None, "lat", "lon"),
            P(),
            P(),
            P(),
        ),
        out_specs=(P("vec", None, None, "lat", "lon"), P()),
        check_vma=False,
    )
```

profile of v0, /device:TPU:0, one launch (start us, length us, event | category | flops | bytes accessed | tf_op | source)
XLA Modules:
  0.0 196.4 jit_solution(7500532654699985628)
XLA Ops:
  9.8 2.1 %select_bitcast_fusion = (bf16[5,48,8,128]{3,1,2,0:T(8,128)(2,1)}, bf16[5,48,8,128]{3,1,2,0:T(8,128)(2,1)}) fusion(pred[]{:T(512)S(6)} %eq.42, bf16[1,5,48,8,128]{4,3,2,1,0:T(8,128)(2,1)} %param.6, pred[]{:T(512)S(6)} %eq.35), kind=kLoop, calls=%fused_computation.63 | loop fusion | flops 491520 | bytes 1474562 | tf_op jit(solution)/shard_map/jit(_where)/select_n | solution.py:14
  13.2 3.0 %collective-permute-start = (bf16[1,5,48,8,1]{4,2,3,1,0:T(8,128)(2,1)}, bf16[1,5,48,8,1]{4,2,3,1,0:T(8,128)(2,1)S(1)}, u32[]{:S(2)}, u32[]{:S(2)}) collective-permute-start(bf16[1,5,48,8,1]{4,2,3,1,0:T(8,128)(2,1)} %get-tuple-element.28), channel_id=1, source_target_pairs={{0,1},{1,2},{2,3},{3,0},{4,5},{5,6},{6,7},{7,4},{8,9},{9,10},{10,1... | collective-permute-start | bytes 11528 | tf_op jit(solution)/shard_map/ppermute | solution.py:25
  16.2 2.0 %collective-permute-start.1 = (bf16[1,5,48,8,1]{4,2,3,1,0:T(8,128)(2,1)S(1)}, bf16[1,5,48,8,1]{4,2,3,1,0:T(8,128)(2,1)}, u32[]{:S(2)}, u32[]{:S(2)}) collective-permute-start(bf16[1,5,48,8,1]{4,2,3,1,0:T(8,128)(2,1)S(1)} %get-tuple-element.29), channel_id=1, source_target_pairs={{1,0},{2,1},{3,2},{0,3},{5,4},{6,5},{7,6},{4,7},{9,8},{10,9},{11,1... | collective-permute-start | bytes 11528 | tf_op jit(solution)/shard_map/ppermute | solution.py:28
  18.9 3.6 %collective-permute-start.2 = (bf16[1,5,48,1,128]{4,2,3,1,0:T(8,128)(2,1)}, bf16[1,5,48,1,128]{4,2,3,1,0:T(8,128)(2,1)S(1)}, u32[]{:S(2)}, u32[]{:S(2)}) collective-permute-start(bf16[1,5,48,1,128]{4,2,3,1,0:T(8,128)(2,1)} %get-tuple-element.30), channel_id=1, source_target_pairs={{0,4},{1,5},{2,6},{3,7},{8,12},{9,13},{10,14},{11,15},{16,20},{17,... | collective-permute-start | bytes 184328 | tf_op jit(solution)/shard_map/ppermute | solution.py:25
  24.2 22.0 %custom-call.7 = f32[5,48,48]{2,1,0:T(8,128)S(1)} custom-call(f32[5,48,48]{2,1,0:T(8,128)S(1)} %fusion.68), custom_call_target="Cholesky" | custom-call | tf_op jit(solution)/shard_map/jit(cholesky)/cholesky | solution.py:47
  46.4 18.5 %custom-call.8 = f32[5,1,48,48]{2,3,1,0:T(8,128)S(1)} custom-call(f32[5,1,48,48]{3,2,1,0:T(8,128)S(1)} %select_bitcast_fusion.2), custom_call_target="InvertDiagBlocksLowerTriangular" | custom-call | tf_op jit(solution)/shard_map/triangular_solve | solution.py:48
  67.5 2.0 %maximum_convert_fusion.4 = f32[1,5,48,10,128]{4,2,3,1,0:T(8,128)} fusion(bf16[1,5,48,1,128]{4,2,3,1,0:T(8,128)(2,1)} %collective-permute-done.3, bf16[1,5,48,8,128]{4,2,3,1,0:T(8,128)(2,1)S(1)} %get-tuple-element.27, bf16[1,5,48,1,128]{4,2,3,1,0:T(8,128)(2,1)S(1)} %collective-permute-done.2), kind=kLoop, calls=%fused_computation.55 | loop fusion | flops 921600 | bytes 1843200 | tf_op jit(solution)/shard_map/convert_element_type | solution.py:81
  71.4 3.8 %collective-permute-start.5 = (bf16[5,48,8,1]{3,1,2,0:T(8,128)(2,1)S(1)}, bf16[5,48,8,1]{3,1,2,0:T(8,128)(2,1)S(1)}, u32[]{:S(2)}, u32[]{:S(2)}) collective-permute-start(bf16[5,48,8,1]{3,1,2,0:T(8,128)(2,1)S(1)} %get-tuple-element.33), channel_id=1, source_target_pairs={{1,0},{2,1},{3,2},{0,3},{5,4},{6,5},{7,6},{4,7},{9,8},{10,9},{11,1... | collective-permute-start | bytes 11528 | tf_op jit(solution)/shard_map/ppermute | solution.py:28
  75.2 5.2 %collective-permute-start.6 = (bf16[5,48,1,128]{3,1,2,0:T(8,128)(2,1)S(1)}, bf16[5,48,1,128]{3,1,2,0:T(8,128)(2,1)S(1)}, u32[]{:S(2)}, u32[]{:S(2)}) collective-permute-start(bf16[5,48,1,128]{3,1,2,0:T(8,128)(2,1)S(1)} %get-tuple-element.34), channel_id=1, source_target_pairs={{0,4},{1,5},{2,6},{3,7},{8,12},{9,13},{10,14},{11,15},{16,20},{17,... | collective-permute-start | bytes 184328 | tf_op jit(solution)/shard_map/ppermute | solution.py:25
  81.8 5.5 %collective-permute-done.4 = bf16[5,48,8,1]{3,1,2,0:T(8,128)(2,1)S(1)} collective-permute-done((bf16[5,48,8,1]{3,1,2,0:T(8,128)(2,1)S(1)}, bf16[5,48,8,1]{3,1,2,0:T(8,128)(2,1)S(1)}, u32[]{:S(2)}, u32[]{:S(2)}) %collective-permute-start.4) | collective-permute-done | bytes 3872 | tf_op jit(solution)/shard_map/ppermute | solution.py:25
  87.4 10.5 %collective-permute-start.13 = (bf16[5,48,8,1]{3,1,2,0:T(8,128)(2,1)S(1)}, bf16[5,48,8,1]{3,1,2,0:T(8,128)(2,1)S(1)}, u32[]{:S(2)}, u32[]{:S(2)}) collective-permute-start(bf16[5,48,8,1]{3,1,2,0:T(8,128)(2,1)S(1)} %get-tuple-element.23), channel_id=1, source_target_pairs={{1,0},{2,1},{3,2},{0,3},{5,4},{6,5},{7,6},{4,7},{9,8},{10,9},{11,1... | collective-permute-start | bytes 11528 | tf_op jit(solution)/shard_map/ppermute | solution.py:28
  98.2 5.4 %collective-permute-start.14 = (bf16[5,48,1,128]{3,1,2,0:T(8,128)(2,1)S(1)}, bf16[5,48,1,128]{3,1,2,0:T(8,128)(2,1)S(1)}, u32[]{:S(2)}, u32[]{:S(2)}) collective-permute-start(bf16[5,48,1,128]{3,1,2,0:T(8,128)(2,1)S(1)} %get-tuple-element.24), channel_id=1, source_target_pairs={{0,4},{1,5},{2,6},{3,7},{8,12},{9,13},{10,14},{11,15},{16,20},{17,... | collective-permute-start | bytes 184328 | tf_op jit(solution)/shard_map/ppermute | solution.py:25
  104.2 4.3 %collective-permute-done.12 = bf16[5,48,8,1]{3,1,2,0:T(8,128)(2,1)S(1)} collective-permute-done((bf16[5,48,8,1]{3,1,2,0:T(8,128)(2,1)S(1)}, bf16[5,48,8,1]{3,1,2,0:T(8,128)(2,1)S(1)}, u32[]{:S(2)}, u32[]{:S(2)}) %collective-permute-start.12) | collective-permute-done | bytes 3872 | tf_op jit(solution)/shard_map/ppermute | solution.py:25
  109.9 5.4 %collective-permute-done.13 = bf16[5,48,8,1]{3,1,2,0:T(8,128)(2,1)S(1)} collective-permute-done((bf16[5,48,8,1]{3,1,2,0:T(8,128)(2,1)S(1)}, bf16[5,48,8,1]{3,1,2,0:T(8,128)(2,1)S(1)}, u32[]{:S(2)}, u32[]{:S(2)}) %collective-permute-start.13) | collective-permute-done | bytes 3872 | tf_op jit(solution)/shard_map/ppermute | solution.py:28
  116.0 1.8 fusion.90
  119.0 2.9 %collective-permute-start.9 = (bf16[1,5,48,8,1]{4,2,3,1,0:T(8,128)(2,1)S(1)}, bf16[1,5,48,8,1]{4,2,3,1,0:T(8,128)(2,1)S(1)}, u32[]{:S(2)}, u32[]{:S(2)}) collective-permute-start(bf16[1,5,48,8,1]{4,2,3,1,0:T(8,128)(2,1)S(1)} %get-tuple-element.19), channel_id=1, source_target_pairs={{1,0},{2,1},{3,2},{0,3},{5,4},{6,5},{7,6},{4,7},{9,8},{10,9},{11,1... | collective-permute-start | bytes 11528 | tf_op jit(solution)/shard_map/ppermute | solution.py:28
  121.9 4.9 %collective-permute-start.10 = (bf16[1,5,48,1,128]{4,2,3,1,0:T(8,128)(2,1)S(1)}, bf16[1,5,48,1,128]{4,2,3,1,0:T(8,128)(2,1)S(1)}, u32[]{:S(2)}, u32[]{:S(2)}) collective-permute-start(bf16[1,5,48,1,128]{4,2,3,1,0:T(8,128)(2,1)S(1)} %get-tuple-element.20), channel_id=1, source_target_pairs={{0,4},{1,5},{2,6},{3,7},{8,12},{9,13},{10,14},{11,15},{16,20},{17,... | collective-permute-start | bytes 184328 | tf_op jit(solution)/shard_map/ppermute | solution.py:25
  128.4 5.6 %collective-permute-done.8 = bf16[1,5,48,8,1]{4,2,3,1,0:T(8,128)(2,1)S(1)} collective-permute-done((bf16[1,5,48,8,1]{4,2,3,1,0:T(8,128)(2,1)S(1)}, bf16[1,5,48,8,1]{4,2,3,1,0:T(8,128)(2,1)S(1)}, u32[]{:S(2)}, u32[]{:S(2)}) %collective-permute-start.8) | collective-permute-done | bytes 3872 | tf_op jit(solution)/shard_map/ppermute | solution.py:25
  134.0 7.0 %collective-permute-done.9 = bf16[1,5,48,8,1]{4,2,3,1,0:T(8,128)(2,1)S(1)} collective-permute-done((bf16[1,5,48,8,1]{4,2,3,1,0:T(8,128)(2,1)S(1)}, bf16[1,5,48,8,1]{4,2,3,1,0:T(8,128)(2,1)S(1)}, u32[]{:S(2)}, u32[]{:S(2)}) %collective-permute-start.9) | collective-permute-done | bytes 3872 | tf_op jit(solution)/shard_map/ppermute | solution.py:28
  141.7 1.8 convolution_bitcast_fusion
  143.7 11.6 %fusion.4 = f32[4,1]{0,1:T(1,128)S(1)} fusion(bf16[4,5,48,8,128]{4,3,2,1,0:T(8,128)(2,1)} %all-gather.3.cloned.1.call-done, f32[5,48,8,128,1]{3,1,2,0,4:T(8,128)S(1)} %multiply_bitcast_fusion), kind=kOutput, calls=%fused_computation.7 | convolution fusion | flops 11796480 | bytes 2949136 | tf_op jit(solution)/shard_map/iflyx,jflyx->ij/dot_general | solution.py:104
  155.2 22.0 %psum.23 = f32[4,1]{0,1:T(1,128)S(1)} all-reduce(f32[4,1]{0,1:T(1,128)S(1)} %fusion.4), channel_id=1, replica_groups=mesh['vec'=4,'lat'=2,'lon'=4] {'lat','lon'}, use_global_device_ids=true, to_apply=%region_4.5 | all-reduce | flops 4 | bytes 32 | tf_op jit(solution)/shard_map/psum | solution.py:107
  177.2 5.2 %fusion = f32[1,5,48,8,128]{4,0,3,2,1:T(1,128)S(1)} fusion(bf16[4,5,48,8,128]{4,3,2,1,0:T(8,128)(2,1)} %all-gather.3.cloned.1.call-done, f32[4,1]{0,1:T(1,128)S(1)} %psum.23), kind=kOutput, calls=%fused_computation | convolution fusion | flops 11796480 | bytes 2949136 | tf_op jit(solution)/shard_map/iflyx,ij->jflyx/dot_general | solution.py:109
  183.9 5.0 %all-gather = f32[4,1,4]{2,1,0:T(1,128)S(1)} all-gather(f32[1,1,4]{2,1,0:T(1,128)S(1)} %bitcast.113), channel_id=1, replica_groups=mesh['vec'=4,'lat'=2,'lon'=4] {'vec'}, dimensions={0}, use_global_device_ids=true | all-gather | bytes 80 | tf_op jit(solution)/shard_map/all_gather | solution.py:108
  (79 shorter events, 19.7 us)
Async XLA Ops:
  7.2 4.9 %copy-start.2 = (bf16[1,5,48,8,128]{4,3,2,1,0:T(8,128)(2,1)S(1)}, bf16[1,5,48,8,128]{4,3,2,1,0:T(8,128)(2,1)}, u32[]{:S(2)}) copy-start(bf16[1,5,48,8,128]{4,3,2,1,0:T(8,128)(2,1)} %param.5) | copy-start | bytes 1474564
  7.2 62.3 %all-reduce.5.cloned.1.call-start = ((), (), s32[]{:S(2)}) async-start(), calls=%async_computation.1 | async-start | bytes 1966080 | tf_op jit(solution)/shard_map/psum | solution.py:15
  12.0 12.0 %copy-start.5 = (f32[5,47]{1,0:T(8,128)S(1)}, f32[5,47]{1,0:T(8,128)}, u32[]{:S(2)}) copy-start(f32[5,47]{1,0:T(8,128)} %param.8) | copy-start | bytes 2824
  12.0 131.7 %all-gather.3.cloned.1.call-start = ((), (), s32[]{:S(2)}) async-start(), calls=%async_computation | async-start | bytes 2457600 | tf_op jit(solution)/shard_map/all_gather | solution.py:97
  12.2 53.2 %copy-start.6 = (f32[5]{0:T(128)S(1)}, f32[5]{0:T(128)}, u32[]{:S(2)}) copy-start(f32[5]{0:T(128)} %param.9) | copy-start | bytes 64
  13.2 52.6 %collective-permute-start = (bf16[1,5,48,8,1]{4,2,3,1,0:T(8,128)(2,1)}, bf16[1,5,48,8,1]{4,2,3,1,0:T(8,128)(2,1)S(1)}, u32[]{:S(2)}, u32[]{:S(2)}) collective-permute-start(bf16[1,5,48,8,1]{4,2,3,1,0:T(8,128)(2,1)} %get-tuple-element.28), channel_id=1, source_target_pairs={{0,1},{1,2},{2,3},{3,0},{4,5},{5,6},{6,7},{7,4},{8,9},{9,10},{10,1... | collective-permute-start | bytes 11528 | tf_op jit(solution)/shard_map/ppermute | solution.py:25
  16.2 49.6 %collective-permute-start.1 = (bf16[1,5,48,8,1]{4,2,3,1,0:T(8,128)(2,1)S(1)}, bf16[1,5,48,8,1]{4,2,3,1,0:T(8,128)(2,1)}, u32[]{:S(2)}, u32[]{:S(2)}) collective-permute-start(bf16[1,5,48,8,1]{4,2,3,1,0:T(8,128)(2,1)S(1)} %get-tuple-element.29), channel_id=1, source_target_pairs={{1,0},{2,1},{3,2},{0,3},{5,4},{6,5},{7,6},{4,7},{9,8},{10,9},{11,1... | collective-permute-start | bytes 11528 | tf_op jit(solution)/shard_map/ppermute | solution.py:28
  18.9 48.6 %collective-permute-start.2 = (bf16[1,5,48,1,128]{4,2,3,1,0:T(8,128)(2,1)}, bf16[1,5,48,1,128]{4,2,3,1,0:T(8,128)(2,1)S(1)}, u32[]{:S(2)}, u32[]{:S(2)}) collective-permute-start(bf16[1,5,48,1,128]{4,2,3,1,0:T(8,128)(2,1)} %get-tuple-element.30), channel_id=1, source_target_pairs={{0,4},{1,5},{2,6},{3,7},{8,12},{9,13},{10,14},{11,15},{16,20},{17,... | collective-permute-start | bytes 184328 | tf_op jit(solution)/shard_map/ppermute | solution.py:25
  22.5 44.9 %collective-permute-start.3 = (bf16[1,5,48,1,128]{4,2,3,1,0:T(8,128)(2,1)}, bf16[1,5,48,1,128]{4,2,3,1,0:T(8,128)(2,1)}, u32[]{:S(2)}, u32[]{:S(2)}) collective-permute-start(bf16[1,5,48,1,128]{4,2,3,1,0:T(8,128)(2,1)} %get-tuple-element.31), channel_id=1, source_target_pairs={{4,0},{5,1},{6,2},{7,3},{12,8},{13,9},{14,10},{15,11},{20,16},{21,... | collective-permute-start | bytes 184328 | tf_op jit(solution)/shard_map/ppermute | solution.py:28
  69.4 1.6 copy-start
  71.4 16.0 %collective-permute-start.4 = (bf16[5,48,8,1]{3,1,2,0:T(8,128)(2,1)S(1)}, bf16[5,48,8,1]{3,1,2,0:T(8,128)(2,1)S(1)}, u32[]{:S(2)}, u32[]{:S(2)}) collective-permute-start(bf16[5,48,8,1]{3,1,2,0:T(8,128)(2,1)S(1)} %get-tuple-element.32), channel_id=1, source_target_pairs={{0,1},{1,2},{2,3},{3,0},{4,5},{5,6},{6,7},{7,4},{8,9},{9,10},{10,1... | collective-permute-start | bytes 11528 | tf_op jit(solution)/shard_map/ppermute | solution.py:25
  71.4 26.8 %collective-permute-start.5 = (bf16[5,48,8,1]{3,1,2,0:T(8,128)(2,1)S(1)}, bf16[5,48,8,1]{3,1,2,0:T(8,128)(2,1)S(1)}, u32[]{:S(2)}, u32[]{:S(2)}) collective-permute-start(bf16[5,48,8,1]{3,1,2,0:T(8,128)(2,1)S(1)} %get-tuple-element.33), channel_id=1, source_target_pairs={{1,0},{2,1},{3,2},{0,3},{5,4},{6,5},{7,6},{4,7},{9,8},{10,9},{11,1... | collective-permute-start | bytes 11528 | tf_op jit(solution)/shard_map/ppermute | solution.py:28
  75.2 40.6 %collective-permute-start.6 = (bf16[5,48,1,128]{3,1,2,0:T(8,128)(2,1)S(1)}, bf16[5,48,1,128]{3,1,2,0:T(8,128)(2,1)S(1)}, u32[]{:S(2)}, u32[]{:S(2)}) collective-permute-start(bf16[5,48,1,128]{3,1,2,0:T(8,128)(2,1)S(1)} %get-tuple-element.34), channel_id=1, source_target_pairs={{0,4},{1,5},{2,6},{3,7},{8,12},{9,13},{10,14},{11,15},{16,20},{17,... | collective-permute-start | bytes 184328 | tf_op jit(solution)/shard_map/ppermute | solution.py:25
  80.4 35.4 %collective-permute-start.7 = (bf16[5,48,1,128]{3,1,2,0:T(8,128)(2,1)S(1)}, bf16[5,48,1,128]{3,1,2,0:T(8,128)(2,1)S(1)}, u32[]{:S(2)}, u32[]{:S(2)}) collective-permute-start(bf16[5,48,1,128]{3,1,2,0:T(8,128)(2,1)S(1)} %get-tuple-element.35), channel_id=1, source_target_pairs={{4,0},{5,1},{6,2},{7,3},{12,8},{13,9},{14,10},{15,11},{20,16},{21,... | collective-permute-start | bytes 184328 | tf_op jit(solution)/shard_map/ppermute | solution.py:28
  81.7 26.8 %collective-permute-start.12 = (bf16[5,48,8,1]{3,1,2,0:T(8,128)(2,1)S(1)}, bf16[5,48,8,1]{3,1,2,0:T(8,128)(2,1)S(1)}, u32[]{:S(2)}, u32[]{:S(2)}) collective-permute-start(bf16[5,48,8,1]{3,1,2,0:T(8,128)(2,1)S(1)} %get-tuple-element.22), channel_id=1, source_target_pairs={{0,1},{1,2},{2,3},{3,0},{4,5},{5,6},{6,7},{7,4},{8,9},{9,10},{10,1... | collective-permute-start | bytes 11528 | tf_op jit(solution)/shard_map/ppermute | solution.py:25
  87.4 27.9 %collective-permute-start.13 = (bf16[5,48,8,1]{3,1,2,0:T(8,128)(2,1)S(1)}, bf16[5,48,8,1]{3,1,2,0:T(8,128)(2,1)S(1)}, u32[]{:S(2)}, u32[]{:S(2)}) collective-permute-start(bf16[5,48,8,1]{3,1,2,0:T(8,128)(2,1)S(1)} %get-tuple-element.23), channel_id=1, source_target_pairs={{1,0},{2,1},{3,2},{0,3},{5,4},{6,5},{7,6},{4,7},{9,8},{10,9},{11,1... | collective-permute-start | bytes 11528 | tf_op jit(solution)/shard_map/ppermute | solution.py:28
  98.2 28.6 %collective-permute-start.14 = (bf16[5,48,1,128]{3,1,2,0:T(8,128)(2,1)S(1)}, bf16[5,48,1,128]{3,1,2,0:T(8,128)(2,1)S(1)}, u32[]{:S(2)}, u32[]{:S(2)}) collective-permute-start(bf16[5,48,1,128]{3,1,2,0:T(8,128)(2,1)S(1)} %get-tuple-element.24), channel_id=1, source_target_pairs={{0,4},{1,5},{2,6},{3,7},{8,12},{9,13},{10,14},{11,15},{16,20},{17,... | collective-permute-start | bytes 184328 | tf_op jit(solution)/shard_map/ppermute | solution.py:25
  108.5 7.5 %copy-start.3 = (bf16[1,5,48,8,128]{4,3,2,1,0:T(8,128)(2,1)S(1)}, bf16[1,5,48,8,128]{4,3,2,1,0:T(8,128)(2,1)}, u32[]{:S(2)}) copy-start(bf16[1,5,48,8,128]{4,3,2,1,0:T(8,128)(2,1)} %param.5) | copy-start | bytes 1474564
  108.5 7.5 %copy-start.4 = (f32[1,5,48,10,128]{4,2,3,1,0:T(8,128)S(1)}, f32[1,5,48,10,128]{4,2,3,1,0:T(8,128)}, u32[]{:S(2)}) copy-start(f32[1,5,48,10,128]{4,2,3,1,0:T(8,128)} %maximum_convert_fusion.4) | copy-start | bytes 3686404
  108.5 19.8 %collective-permute-start.15 = (bf16[5,48,1,128]{3,1,2,0:T(8,128)(2,1)S(1)}, bf16[5,48,1,128]{3,1,2,0:T(8,128)(2,1)S(1)}, u32[]{:S(2)}, u32[]{:S(2)}) collective-permute-start(bf16[5,48,1,128]{3,1,2,0:T(8,128)(2,1)S(1)} %get-tuple-element.25), channel_id=1, source_target_pairs={{4,0},{5,1},{6,2},{7,3},{12,8},{13,9},{14,10},{15,11},{20,16},{21,... | collective-permute-start | bytes 184328 | tf_op jit(solution)/shard_map/ppermute | solution.py:28
  118.0 16.0 %collective-permute-start.8 = (bf16[1,5,48,8,1]{4,2,3,1,0:T(8,128)(2,1)S(1)}, bf16[1,5,48,8,1]{4,2,3,1,0:T(8,128)(2,1)S(1)}, u32[]{:S(2)}, u32[]{:S(2)}) collective-permute-start(bf16[1,5,48,8,1]{4,2,3,1,0:T(8,128)(2,1)S(1)} %get-tuple-element.18), channel_id=1, source_target_pairs={{0,1},{1,2},{2,3},{3,0},{4,5},{5,6},{6,7},{7,4},{8,9},{9,10},{10,1... | collective-permute-start | bytes 11528 | tf_op jit(solution)/shard_map/ppermute | solution.py:25
  119.0 22.0 %collective-permute-start.9 = (bf16[1,5,48,8,1]{4,2,3,1,0:T(8,128)(2,1)S(1)}, bf16[1,5,48,8,1]{4,2,3,1,0:T(8,128)(2,1)S(1)}, u32[]{:S(2)}, u32[]{:S(2)}) collective-permute-start(bf16[1,5,48,8,1]{4,2,3,1,0:T(8,128)(2,1)S(1)} %get-tuple-element.19), channel_id=1, source_target_pairs={{1,0},{2,1},{3,2},{0,3},{5,4},{6,5},{7,6},{4,7},{9,8},{10,9},{11,1... | collective-permute-start | bytes 11528 | tf_op jit(solution)/shard_map/ppermute | solution.py:28
  121.9 19.7 %collective-permute-start.10 = (bf16[1,5,48,1,128]{4,2,3,1,0:T(8,128)(2,1)S(1)}, bf16[1,5,48,1,128]{4,2,3,1,0:T(8,128)(2,1)S(1)}, u32[]{:S(2)}, u32[]{:S(2)}) collective-permute-start(bf16[1,5,48,1,128]{4,2,3,1,0:T(8,128)(2,1)S(1)} %get-tuple-element.20), channel_id=1, source_target_pairs={{0,4},{1,5},{2,6},{3,7},{8,12},{9,13},{10,14},{11,15},{16,20},{17,... | collective-permute-start | bytes 184328 | tf_op jit(solution)/shard_map/ppermute | solution.py:25
  126.8 14.7 %collective-permute-start.11 = (bf16[1,5,48,1,128]{4,2,3,1,0:T(8,128)(2,1)S(1)}, bf16[1,5,48,1,128]{4,2,3,1,0:T(8,128)(2,1)S(1)}, u32[]{:S(2)}, u32[]{:S(2)}) collective-permute-start(bf16[1,5,48,1,128]{4,2,3,1,0:T(8,128)(2,1)S(1)} %get-tuple-element.21), channel_id=1, source_target_pairs={{4,0},{5,1},{6,2},{7,3},{12,8},{13,9},{14,10},{15,11},{20,16},{21,... | collective-permute-start | bytes 184328 | tf_op jit(solution)/shard_map/ppermute | solution.py:28
  (1 other events, 1.5 us)
Sparse Core Ops, SparseCore 0:
  12.1 38.7 all-reduce.4
  52.5 22.6 all-gather.2
where the time goes:
time: 197 us; the launch traced here: 196 us
  other arithmetic  49.5 us (25%)
  starting transfers between devices  48 us (24%)
  waiting for transfers between devices  28.1 us (14%)
  blocking collectives  27 us (14%)
  matrix products  21.2 us (11%)
  between operations  15.9 us (8%)
  local copies, waits for them, and re-layouts  6.82 us (3%)
    ppermute x8, starting transfers between devices, with_halo(): lax.ppermute(lax.slice_in_dim(block, 0, width, axis=dim), axis, backward)  24.7 us
    ppermute x8, starting transfers between devices, with_halo(): lax.ppermute(lax.slice_in_dim(block, block.shape[dim] - width, None, axis...  23.2 us
    another operation x4, other arithmetic, implicit_inverse(): factor = jnp.linalg.cholesky(matrix)  22.1 us
    psum x1, blocking collectives, per_device(): own_columns = lax.psum(partial_gram, ('lat', 'lon'))  22 us
    another operation x3, other arithmetic, implicit_inverse(): lax.linalg.triangular_solve(factor, jnp.broadcast_to(identity_mat, matrix...  18.5 us
    ppermute x8, waiting for transfers between devices, with_halo(): lax.ppermute(lax.slice_in_dim(block, block.shape[dim] - width, None, axis...  15.4 us
    ppermute x8, waiting for transfers between devices, with_halo(): lax.ppermute(lax.slice_in_dim(block, 0, width, axis=dim), axis, backward)  12.7 us
    dot_general x1, matrix products, per_device(): jnp.einsum('iflyx,jflyx->ij', all_basis, weighted, precision=HIGH, prefer...  11.6 us
  transfers between devices with their start and end apart: 18, of which 6 were waited for; matrix products, arithmetic and copies ran while one was open for 28% of the time, Pallas kernels for 0%

commit v1 on v0

v1 whole, which is shorter than its diff:
```python
import functools
import math

import jax
import jax.numpy as jnp
from jax import lax
from jax.experimental import pallas as pl
from jax.experimental.pallas import tpu as pltpu
from jax.sharding import PartitionSpec as P

STEPS = 2
COURANT = 0.25
MESH = pl.DeviceIdType.MESH
F32 = jnp.float32
BF16 = jnp.bfloat16


def copy_names(pairs, tiles, groups):
    names = ["traj", "basis"]
    for d in range(1, pairs):
        names += [(kind, k, d) for kind in ("cross", "relay") for k in range(2)]
        names += [(kind, t, d) for kind in ("slice", "pass") for t in range(STEPS)]
    for t in range(STEPS):
        names += [(kind, t, s) for kind in ("flon", "flat", "slon", "slat") for s in range(2)]
    names += [("sum", k) for k in range(1, tiles)]
    names += [("col", k) for k in range(1, groups)]
    return {name: i for i, name in enumerate(names)}


def kernel(
    shape,
    counts,
    ids,
    basis_ref,
    traj_ref,
    owner_ref,
    diff_ref,
    weight_ref,
    out_ref,
    coup_ref,
    sib_traj,
    sel,
    rcv,
    allb,
    field,
    state,
    coef,
    lon_out,
    lon_in,
    lat_out,
    lat_in,
    lon_mix,
    sums,
    cols,
    send_sem,
    recv_sem,
):
    fields, levels, rows, lanes = shape
    groups, lats, lons = counts
    pairs, tiles = groups // 2, lats * lons
    size = fields * levels * rows
    per_field = levels * rows
    half = size // 2
    vec = lax.axis_index("vec")
    lat = lax.axis_index("lat")
    lon = lax.axis_index("lon")
    core = lax.rem(vec, 2)
    pair = vec // 2
    sibling = vec + 1 - 2 * core
    me = lat * lons + lon

    def other_tile(k):
        index = lax.rem(me + k, tiles)
        return {"lat": index // lons, "lon": lax.rem(index, lons)}

    def other_vec(k):
        return {"vec": lax.rem(vec + k, groups)}

    def partner(d):
        return {"vec": 2 * lax.rem(pair + d, pairs) + core}

    def remote(name, src, dst, device):
        return pltpu.make_async_remote_copy(
            src_ref=src,
            dst_ref=dst,
            send_sem=send_sem.at[ids[name]],
            recv_sem=recv_sem.at[ids[name]],
            device_id=device,
            device_id_type=MESH,
        )

    barrier = pltpu.get_barrier_semaphore()
    for k in range(1, tiles):
        pl.semaphore_signal(barrier, inc=1, device_id=other_tile(k), device_id_type=MESH)
    for k in range(1, groups):
        pl.semaphore_signal(barrier, inc=1, device_id=other_vec(k), device_id_type=MESH)
    pl.semaphore_wait(barrier, tiles + groups - 2)

    parts = ((0, per_field), (per_field, size - per_field))
    to_sibling = {"vec": sibling}
    own_half = pl.ds(pl.multiple_of(core * half, 16), half)

    traj_copy = remote("traj", traj_ref, sib_traj, to_sibling)
    traj_copy.start()
    cross = {}
    relay = {}
    for d in range(1, pairs):
        source = 2 * lax.rem(pair + pairs - d, pairs) + core
        for k, (first, count) in enumerate(parts):
            chunk = pl.ds(first, count)
            cross[k, d] = remote(
                ("cross", k, d), basis_ref.at[chunk], allb.at[vec, chunk], partner(d)
            )
            relay[k, d] = remote(
                ("relay", k, d), allb.at[source, chunk], allb.at[source, chunk], to_sibling
            )
    for d in range(1, pairs):
        cross[0, d].start()
    basis_copy = remote("basis", basis_ref, allb.at[vec], to_sibling)
    basis_copy.start()

    lane = lax.broadcasted_iota(jnp.int32, (rows, lanes), 1)
    row = lax.broadcasted_iota(jnp.int32, (rows, lanes), 0)

    def edge_copies(kind, slot, t):
        east = {"lon": lax.rem(lon + 1, lons)}
        west = {"lon": lax.rem(lon + lons - 1, lons)}
        up = {"lat": lax.rem(lat + 1, lats)}
        down = {"lat": lax.rem(lat + lats - 1, lats)}
        return (
            remote((kind + "lon", t, 0), lon_out.at[slot], lon_in.at[slot, 0], east),
            remote((kind + "lon", t, 1), lon_out.at[slot], lon_in.at[slot, 1], west),
            remote((kind + "lat", t, 0), lat_out.at[slot, 1], lat_in.at[slot, 0], up),
            remote((kind + "lat", t, 1), lat_out.at[slot, 0], lat_in.at[slot, 1], down),
        )

    def start_edges(copies):
        copies[0].start()
        copies[1].start()

        @pl.when(lat < lats - 1)
        def _():
            copies[2].start()

        @pl.when(lat > 0)
        def _():
            copies[3].start()

    def await_edges(copies, slot):
        copies[0].wait_recv()
        copies[1].wait_recv()

        @pl.when(lat > 0)
        def _():
            copies[2].wait_recv()

        @pl.when(lat < lats - 1)
        def _():
            copies[3].wait_recv()

        for f in range(fields):
            lon_mix[slot, f] = jnp.where(
                lax.rem(lane, 2) == 0,
                pltpu.roll(lon_in[slot, 0, f], 1, 1),
                pltpu.roll(lon_in[slot, 1, f], lanes - 1, 1),
            )

    def await_edges_sent(copies):
        copies[0].wait_send()
        copies[1].wait_send()

        @pl.when(lat < lats - 1)
        def _():
            copies[2].wait_send()

        @pl.when(lat > 0)
        def _():
            copies[3].wait_send()

    def note_edges(slot, f, level, tile, packed):
        lat_out[slot, 0, f, level] = tile[0:1]
        lat_out[slot, 1, f, level] = tile[rows - 1 : rows]
        spot = 2 * level
        here = (lane == spot) | (lane == lax.rem(spot + lanes - 1, lanes))
        return jnp.where(here, pltpu.roll(tile, spot, 1), packed)

    no_tiles = tuple(jnp.zeros((rows, lanes), F32) for _ in range(fields))

    def spread(load, store, slot):
        def body(m, packed):
            done = []
            for f in range(fields):
                first = pl.multiple_of(f * per_field + m * 2 * rows, 2 * rows)
                both = load(pl.ds(first, 2 * rows))
                p = packed[f]
                for i in range(2):
                    tile = both[i * rows : (i + 1) * rows]
                    store(f, 2 * m + i, tile)
                    p = note_edges(slot, f, 2 * m + i, tile, p)
                done.append(p)
            return tuple(done)

        packed = lax.fori_loop(0, levels // 2, body, no_tiles)
        for f in range(fields):
            lon_out[slot, f] = packed[f]

    for slot in range(2 * STEPS):

        @pl.when(lat == 0)
        def _():
            lat_in[slot, 0] = jnp.zeros((fields, levels, 1, lanes), F32)

        @pl.when(lat == lats - 1)
        def _():
            lat_in[slot, 1] = jnp.zeros((fields, levels, 1, lanes), F32)

    def load_basis(where):
        block = basis_ref[where, :]
        allb[vec, where, :] = block
        return block.astype(F32)

    def store_field(f, level, tile):
        field[f, level] = tile

    spread(load_basis, store_field, 0)
    field_edges = [edge_copies("f", t, t) for t in range(STEPS)]
    state_edges = [edge_copies("s", STEPS + t, t) for t in range(STEPS)]
    start_edges(field_edges[0])

    traj_copy.wait_recv()
    slices = {}
    passes = {}
    for t in range(STEPS):
        sel[t] = jnp.where(
            owner_ref[t] == vec, traj_ref[...].astype(F32), sib_traj[...].astype(F32)
        ).astype(BF16)
        for d in range(1, pairs):
            slices[t, d] = remote(
                ("slice", t, d), sel.at[t, own_half], rcv.at[t, d - 1, own_half], partner(d)
            )
            passes[t, d] = remote(
                ("pass", t, d), rcv.at[t, d - 1, own_half], rcv.at[t, d - 1, own_half], to_sibling
            )
            slices[t, d].start()

    def pivots(level, carry):
        done = []
        for f in range(fields):
            above, ratio = carry[f]
            below = jnp.full((rows, lanes), diff_ref[f, level], F32)
            inv = 1.0 / (1.0 + below + above - above * ratio)
            coef[0, f, level] = inv
            coef[1, f, level] = above * inv
            coef[2, f, level] = below * inv
            done.append((below, below * inv))
        return tuple(done)

    zero = jnp.zeros((rows, lanes), F32)
    carry = lax.fori_loop(0, levels - 1, pivots, tuple((zero, zero) for _ in range(fields)))
    for f in range(fields):
        above, ratio = carry[f]
        inv = 1.0 / (1.0 + above - above * ratio)
        coef[0, f, levels - 1] = inv
        coef[1, f, levels - 1] = above * inv
        coef[2, f, levels - 1] = zero

    def take_state(t):
        for d in range(1, pairs):
            slices[t, d].wait_recv()
            passes[t, d].start()

    def build_state(t):
        for d in range(1, pairs):
            passes[t, d].wait_recv()
        holder = owner_ref[t] // 2

        def load_state(where):
            block = sel[t, where, :].astype(F32)
            for d in range(1, pairs):
                source = lax.rem(pair + pairs - d, pairs)
                block = jnp.where(holder == source, rcv[t, d - 1, where, :].astype(F32), block)
            return block

        def store_state(f, level, tile):
            state[t, f, level] = tile

        spread(load_state, store_state, STEPS + t)
        start_edges(state_edges[t])

    def dlon(tile, mix, shift):
        mix = pltpu.roll(mix, shift, 1)
        after = jnp.where(lane == lanes - 1, mix, pltpu.roll(tile, lanes - 1, 1))
        before = jnp.where(lane == 0, mix, pltpu.roll(tile, 1, 1))
        return after - before

    def dlat(tile, low, high):
        after = jnp.where(row == rows - 1, high, pltpu.roll(tile, rows - 1, 0))
        before = jnp.where(row == 0, low, pltpu.roll(tile, 1, 0))
        return after - before

    def step(t):
        fslot, sslot = t, STEPS + t

        def forward(level, solved):
            wind_u, wind_v = state[t, 0, level], state[t, 1, level]
            pert_u, pert_v = field[0, level], field[1, level]
            shift = lax.rem(lanes - 2 * level, lanes)
            done = []
            for f in range(fields):
                a, s = field[f, level], state[t, f, level]
                change = wind_u * dlon(a, lon_mix[fslot, f], shift)
                change += wind_v * dlat(a, lat_in[fslot, 0, f, level], lat_in[fslot, 1, f, level])
                change += pert_u * dlon(s, lon_mix[sslot, f], shift)
                change += pert_v * dlat(s, lat_in[sslot, 0, f, level], lat_in[sslot, 1, f, level])
                moved = a - (0.5 * COURANT) * change
                done.append(moved * coef[0, f, level] + solved[f] * coef[1, f, level])
            for f in range(fields):
                field[f, level] = done[f]
            return tuple(done)

        lax.fori_loop(0, levels, forward, no_tiles)
        last = t == STEPS - 1

        def backward(k, carry):
            level = levels - 1 - k
            above, packed = carry
            done, edges = [], []
            for f in range(fields):
                x = field[f, level] + coef[2, f, level] * above[f]
                field[f, level] = x
                done.append(x)
                if not last:
                    edges.append(note_edges(t + 1, f, level, x, packed[f]))
            return tuple(done), tuple(edges)

        _, packed = lax.fori_loop(0, levels, backward, (no_tiles, () if last else no_tiles))
        if not last:
            for f in range(fields):
                lon_out[t + 1, f] = packed[f]
            start_edges(field_edges[t + 1])

    for t in range(STEPS):
        take_state(t)
        if t == 0:
            for d in range(1, pairs):
                cross[1, d].start()
        build_state(t)
        if t == 0:
            for d in range(1, pairs):
                cross[0, d].wait_recv()
                relay[0, d].start()
        await_edges(field_edges[t], t)
        await_edges(state_edges[t], STEPS + t)
        step(t)

    basis_copy.wait_recv()
    for d in range(1, pairs):
        cross[1, d].wait_recv()
        relay[1, d].start()
    for d in range(1, pairs):
        relay[0, d].wait_recv()
        relay[1, d].wait_recv()

    total_rows = rows * lats
    total = float(fields * levels * total_rows * lanes * lons)
    row_ids = (lat * rows + row).astype(F32)
    cosine = jnp.cos((row_ids + 0.5) * (math.pi / total_rows) - math.pi / 2)

    def load_vector(i, f, m):
        first = pl.multiple_of(f * per_field + m * 2 * rows, 2 * rows)
        return allb[i, pl.ds(first, 2 * rows), :].astype(F32)

    def gram(m, acc):
        acc = list(acc)
        for f in range(fields):
            scale = weight_ref[f] * cosine / total
            low = field[f, 2 * m] * scale
            high = field[f, 2 * m + 1] * scale
            for i in range(groups):
                b = load_vector(i, f, m)
                acc[i] += b[:rows] * low + b[rows:] * high
        return tuple(acc)

    acc = lax.fori_loop(0, levels // 2, gram, tuple(zero for _ in range(groups)))
    part = jnp.zeros((8, lanes), F32)
    part_row = lax.broadcasted_iota(jnp.int32, (8, lanes), 0)
    for i in range(groups):
        part = jnp.where(part_row == i, jnp.sum(acc[i], axis=0, keepdims=True), part)
    sums[me] = part
    sum_copies = []
    for k in range(1, tiles):
        copy = remote(("sum", k), sums.at[me], sums.at[me], other_tile(k))
        copy.start()
        sum_copies.append(copy)
    for copy in sum_copies:
        copy.wait_recv()
    whole = sums[0]
    for k in range(1, tiles):
        whole += sums[k]
    column = jnp.sum(whole, axis=1, keepdims=True)
    cols[vec] = jnp.broadcast_to(column, (8, lanes))
    col_copies = []
    for k in range(1, groups):
        copy = remote(("col", k), cols.at[vec], cols.at[vec], other_vec(k))
        copy.start()
        col_copies.append(copy)
    factor = [jnp.broadcast_to(column[i : i + 1], (rows, lanes)) for i in range(groups)]

    def residual(m, carry):
        for f in range(fields):
            low, high = field[f, 2 * m], field[f, 2 * m + 1]
            for i in range(groups):
                b = load_vector(i, f, m)
                low -= b[:rows] * factor[i]
                high -= b[rows:] * factor[i]
            out_ref[f, 2 * m] = low
            out_ref[f, 2 * m + 1] = high
        return carry

    lax.fori_loop(0, levels // 2, residual, 0)
    for copy in col_copies:
        copy.wait_recv()
    table = jnp.zeros((8, lanes), F32)
    wide_lane = lax.broadcasted_iota(jnp.int32, (8, lanes), 1)
    for j in range(groups):
        table = jnp.where(wide_lane == j, cols[j], table)
    coup_ref[...] = table[:groups, :groups]

    traj_copy.wait_send()
    basis_copy.wait_send()
    for d in range(1, pairs):
        for k in range(2):
            cross[k, d].wait_send()
            relay[k, d].wait_send()
        for t in range(STEPS):
            slices[t, d].wait_send()
            passes[t, d].wait_send()
    for t in range(STEPS):
        await_edges_sent(field_edges[t])
        await_edges_sent(state_edges[t])
    for copy in sum_copies + col_copies:
        copy.wait_send()


def solution(mesh):
    groups, lats, lons = mesh.shape["vec"], mesh.shape["lat"], mesh.shape["lon"]

    def per_device(basis, trajectory, slice_owner, diffusion, energy_weight):
        _, fields, levels, rows, lanes = basis.shape
        size = fields * levels * rows
        pairs, tiles = groups // 2, lats * lons
        ids = copy_names(pairs, tiles, groups)
        slots = 2 * STEPS
        vmem = pl.BlockSpec(memory_space=pltpu.VMEM)
        smem = pl.BlockSpec(memory_space=pltpu.SMEM)
        residual_block, coupling = pl.pallas_call(
            functools.partial(kernel, (fields, levels, rows, lanes), (groups, lats, lons), ids),
            out_shape=(
                jax.ShapeDtypeStruct((fields, levels, rows, lanes), F32),
                jax.ShapeDtypeStruct((groups, groups), F32),
            ),
            in_specs=[vmem, vmem, smem, smem, smem],
            out_specs=(vmem, vmem),
            scratch_shapes=[
                pltpu.VMEM((size, lanes), BF16),
                pltpu.VMEM((STEPS, size, lanes), BF16),
                pltpu.VMEM((STEPS, max(pairs - 1, 1), size, lanes), BF16),
                pltpu.VMEM((groups, size, lanes), BF16),
                pltpu.VMEM((fields, levels, rows, lanes), F32),
                pltpu.VMEM((STEPS, fields, levels, rows, lanes), F32),
                pltpu.VMEM((3, fields, levels, rows, lanes), F32),
                pltpu.VMEM((slots, fields, rows, lanes), F32),
                pltpu.VMEM((slots, 2, fields, rows, lanes), F32),
                pltpu.VMEM((slots, 2, fields, levels, 1, lanes), F32),
                pltpu.VMEM((slots, 2, fields, levels, 1, lanes), F32),
                pltpu.VMEM((slots, fields, rows, lanes), F32),
                pltpu.VMEM((tiles, 8, lanes), F32),
                pltpu.VMEM((groups, 8, lanes), F32),
                pltpu.SemaphoreType.DMA((len(ids),)),
                pltpu.SemaphoreType.DMA((len(ids),)),
            ],
            compiler_params=pltpu.CompilerParams(
                collective_id=0, has_side_effects=True, vmem_limit_bytes=48 * 1024 * 1024
            ),
        )(
            basis.reshape(size, lanes),
            trajectory.reshape(size, lanes),
            slice_owner,
            diffusion,
            energy_weight,
        )
        return residual_block[None], coupling

    return jax.shard_map(
        per_device,
        mesh=mesh,
        in_specs=(
            P("vec", None, None, "lat", "lon"),
            P("vec", None, None, "lat", "lon"),
            P(),
            P(),
            P(),
        ),
        out_specs=(P("vec", None, None, "lat", "lon"), P()),
        check_vma=False,
    )
```

time: 197 us -> 59.9 us (0.30)
  Pallas kernels: 0 us -> 54.1 us
  other arithmetic: 49.5 us -> 0 us
  starting transfers between devices: 48 us -> 0 us
  waiting for transfers between devices: 28.1 us -> 0 us
  blocking collectives: 27 us -> 0 us
  matrix products: 21.2 us -> 0 us
  between operations: 15.9 us -> 0.66 us
    pallas_call x0 -> x1, Pallas kernels: none -> 54.1 us  [per_device(): pl.pallas_call(functools.partial(kernel, (fields, levels, rows, lanes), (...]
    ppermute x16 -> x0, starting transfers between devices: 47.9 us -> none  [the longest x8 24.7 us: with_halo(): lax.ppermute(lax.slice_in_dim(block, 0, width, axis=dim), axis, backward)]
    another operation x8 -> x0, other arithmetic: 40.8 us -> none  [the longest x4 22.1 us: implicit_inverse(): factor = jnp.linalg.cholesky(matrix)]
    ppermute x16 -> x0, waiting for transfers between devices: 28.1 us -> none  [the longest x8 15.4 us: with_halo(): lax.ppermute(lax.slice_in_dim(block, block.shape[dim] - width, None, axis...]
    psum x1 -> x0, blocking collectives: 22 us -> none  [per_device(): own_columns = lax.psum(partial_gram, ('lat', 'lon'))]
    dot_general x5 -> x0, matrix products: 20.8 us -> none  [the longest x1 11.6 us: per_device(): jnp.einsum('iflyx,jflyx->ij', all_basis, weighted, precision=HIGH, prefer...]
    convert_element_type x13 -> x0, other arithmetic: 5.89 us -> none  [the longest x2 2.14 us: per_device(): with_halo(field.astype(jnp.bfloat16), (('lon', 4),), 1, True)]
    all_gather x1 -> x0, blocking collectives: 5.03 us -> none  [per_device(): coupling = lax.all_gather(own_columns, 'vec', axis=1, tiled=True)]
  transfers between devices with their start and end apart: 18 -> 0, of which waited for: 6 -> 0; matrix products, arithmetic and copies ran while one was open for 28% -> 0% of each run, Pallas kernels for 0% -> 0%
where the time goes in v1:
time: 59.9 us; the launch traced here: 59.7 us
  Pallas kernels  54.1 us (90%)
  local copies, waits for them, and re-layouts  4.93 us (8%)
  between operations  0.66 us (1%)
    pallas_call x1, Pallas kernels, per_device(): pl.pallas_call(functools.partial(kernel, (fields, levels, rows, lanes), (...  54.1 us
    unnamed x12, local copies, waits for them, and re-layouts  4.93 us

profile of v1, /device:TPU:0, one launch (start us, length us, event | category | flops | bytes accessed | tf_op | source)
XLA Modules:
  0.0 59.7 jit_solution(17784654662537677683)
XLA Ops:
  0.6 0.0 copy-start.3
  0.6 0.0 copy-start.4
  0.7 0.6 %copy-done.3 = s32[4]{0:T(128)S(1)} copy-done((s32[4]{0:T(128)S(1)}, s32[4]{0:T(128)}, u32[]{:S(2)}) %copy-start.3) | copy-done | bytes 40
  1.3 0.0 copy-done.4
  1.3 0.0 copy-start
  1.3 1.0 %copy-done = bf16[1,5,48,8,128]{4,3,2,1,0:T(8,128)(2,1)S(1)} copy-done((bf16[1,5,48,8,128]{4,3,2,1,0:T(8,128)(2,1)S(1)}, bf16[1,5,48,8,128]{4,3,2,1,0:T(8,128)(2,1)}, u32[]{:S(2)}) %copy-start) | copy-done | bytes 491544
  2.3 0.0 copy-start.1
  2.3 1.0 %copy-done.1 = bf16[1,5,48,8,128]{4,3,2,1,0:T(8,128)(2,1)S(1)} copy-done((bf16[1,5,48,8,128]{4,3,2,1,0:T(8,128)(2,1)S(1)}, bf16[1,5,48,8,128]{4,3,2,1,0:T(8,128)(2,1)}, u32[]{:S(2)}) %copy-start.1) | copy-done | bytes 491544
  3.4 0.0 copy-start.2
  3.4 0.7 %copy-done.2 = f32[5,47]{1,0:T(8,128)S(1)} copy-done((f32[5,47]{1,0:T(8,128)S(1)}, f32[5,47]{1,0:T(8,128)}, u32[]{:S(2)}) %copy-start.2) | copy-done | bytes 964
  4.1 54.1 %shard_map.68 = (f32[5,48,8,128]{3,2,1,0:T(8,128)S(1)}, f32[4,4]{1,0:T(4,128)S(1)}) custom-call(bf16[1920,128]{1,0:T(8,128)(2,1)S(1)} %bitcast.4, bf16[1920,128]{1,0:T(8,128)(2,1)S(1)} %bitcast.5, s32[4]{0:T(128)S(1)} %copy-done.3, f32[5,47]{1,0:T(8,128)S(1)} %copy-done.2, f32[5]{0:T(128)S(1)} %copy-done.4), custom_call_target="tpu_custom_call" | custom-call | tf_op jit(solution)/shard_map/pallas_call | solution.py:456
  58.1 0.9 %copy.9 = f32[1,5,48,8,128]{4,3,2,1,0:T(8,128)} copy(f32[1,5,48,8,128]{4,3,2,1,0:T(8,128)S(1)} %bitcast.3) | data formatting | bytes 1966080
  59.1 0.6 copy.10
Async XLA Ops:
  0.6 0.7 %copy-start.3 = (s32[4]{0:T(128)S(1)}, s32[4]{0:T(128)}, u32[]{:S(2)}) copy-start(s32[4]{0:T(128)} %owner_ref.1) | copy-start | bytes 52
  0.6 0.7 %copy-start.4 = (f32[5]{0:T(128)S(1)}, f32[5]{0:T(128)}, u32[]{:S(2)}) copy-start(f32[5]{0:T(128)} %weight_ref.1) | copy-start | bytes 64
  1.3 1.0 %copy-start = (bf16[1,5,48,8,128]{4,3,2,1,0:T(8,128)(2,1)S(1)}, bf16[1,5,48,8,128]{4,3,2,1,0:T(8,128)(2,1)}, u32[]{:S(2)}) copy-start(bf16[1,5,48,8,128]{4,3,2,1,0:T(8,128)(2,1)} %param.5) | copy-start | bytes 1474564
  2.3 1.0 %copy-start.1 = (bf16[1,5,48,8,128]{4,3,2,1,0:T(8,128)(2,1)S(1)}, bf16[1,5,48,8,128]{4,3,2,1,0:T(8,128)(2,1)}, u32[]{:S(2)}) copy-start(bf16[1,5,48,8,128]{4,3,2,1,0:T(8,128)(2,1)} %param.6) | copy-start | bytes 1474564
  3.4 0.7 %copy-start.2 = (f32[5,47]{1,0:T(8,128)S(1)}, f32[5,47]{1,0:T(8,128)}, u32[]{:S(2)}) copy-start(f32[5,47]{1,0:T(8,128)} %diff_ref.1) | copy-start | bytes 2824

commit v2 on v1

v2 whole, which is shorter than its diff:
```python
import functools
import math

import jax
import jax.numpy as jnp
from jax import lax
from jax.experimental import pallas as pl
from jax.experimental.pallas import tpu as pltpu
from jax.sharding import PartitionSpec as P

STEPS = 2
COURANT = 0.25
MESH = pl.DeviceIdType.MESH
F32 = jnp.float32
BF16 = jnp.bfloat16


def copy_names(pairs, tiles, groups, fields):
    names = [("traj", 0), ("traj", 1), "basis"]
    for d in range(1, pairs):
        names += [(kind, k, d) for kind in ("cross", "relay") for k in range(fields)]
        names += [(kind, t, d) for kind in ("slice", "pass") for t in range(STEPS)]
    for t in range(STEPS):
        names += [(kind, t, s) for kind in ("flon", "flat", "slon", "slat") for s in range(2)]
    names += [("sum", k) for k in range(1, tiles)]
    names += [("col", k) for k in range(1, groups)]
    return {name: i for i, name in enumerate(names)}


def kernel(
    shape,
    counts,
    ids,
    basis_ref,
    traj_ref,
    owner_in,
    diff_in,
    weight_in,
    out_ref,
    coup_ref,
    owner_ref,
    diff_ref,
    weight_ref,
    own_traj,
    sib_traj,
    sel,
    rcv,
    allb,
    field,
    state,
    coef,
    lon_out,
    lon_in,
    lat_out,
    lat_in,
    lat_wide,
    lon_mix,
    lat_rows,
    sums,
    cols,
    local_sem,
    send_sem,
    recv_sem,
):
    fields, levels, rows, lanes = shape
    groups, lats, lons = counts
    pairs, tiles = groups // 2, lats * lons
    size = fields * levels * rows
    per_field = levels * rows
    half = size // 2
    vec = lax.axis_index("vec")
    lat = lax.axis_index("lat")
    lon = lax.axis_index("lon")
    core = lax.rem(vec, 2)
    pair = vec // 2
    sibling = vec + 1 - 2 * core
    me = lat * lons + lon

    def other_tile(k):
        index = lax.rem(me + k, tiles)
        return {"lat": index // lons, "lon": lax.rem(index, lons)}

    def other_vec(k):
        return {"vec": lax.rem(vec + k, groups)}

    def partner(d):
        return {"vec": 2 * lax.rem(pair + d, pairs) + core}

    def remote(name, src, dst, device):
        return pltpu.make_async_remote_copy(
            src_ref=src,
            dst_ref=dst,
            send_sem=send_sem.at[ids[name]],
            recv_sem=recv_sem.at[ids[name]],
            device_id=device,
            device_id_type=MESH,
        )

    local = [
        pltpu.make_async_copy(source, target, local_sem.at[i])
        for i, (source, target) in enumerate(
            (
                (basis_ref, allb.at[vec]),
                (traj_ref, own_traj),
                (owner_in, owner_ref),
                (diff_in, diff_ref),
                (weight_in, weight_ref),
            )
        )
    ]
    for copy in local:
        copy.start()

    barrier = pltpu.get_barrier_semaphore()
    for k in range(1, tiles):
        pl.semaphore_signal(barrier, inc=1, device_id=other_tile(k), device_id_type=MESH)
    for k in range(1, groups):
        pl.semaphore_signal(barrier, inc=1, device_id=other_vec(k), device_id_type=MESH)
    pl.semaphore_wait(barrier, tiles + groups - 2)

    to_sibling = {"vec": sibling}
    own_half = pl.ds(pl.multiple_of(core * half, 16), half)
    far_half = pl.ds(pl.multiple_of((1 - core) * half, 16), half)

    traj_copies = [
        remote(("traj", i), traj_ref.at[part], sib_traj.at[part], to_sibling)
        for i, part in enumerate((far_half, own_half))
    ]
    traj_copies[0].start()
    cross = {}
    relay = {}
    for d in range(1, pairs):
        source = 2 * lax.rem(pair + pairs - d, pairs) + core
        for f in range(fields):
            chunk = pl.ds(f * per_field, per_field)
            cross[f, d] = remote(
                ("cross", f, d), basis_ref.at[chunk], allb.at[vec, chunk], partner(d)
            )
            relay[f, d] = remote(
                ("relay", f, d), allb.at[source, chunk], allb.at[source, chunk], to_sibling
            )
    for d in range(1, pairs):
        cross[0, d].start()
    traj_copies[1].start()
    basis_copy = remote("basis", basis_ref, allb.at[vec], to_sibling)
    basis_copy.start()

    lane = lax.broadcasted_iota(jnp.int32, (rows, lanes), 1)
    row = lax.broadcasted_iota(jnp.int32, (rows, lanes), 0)

    def edge_copies(kind, slot, t):
        east = {"lon": lax.rem(lon + 1, lons)}
        west = {"lon": lax.rem(lon + lons - 1, lons)}
        up = {"lat": lax.rem(lat + 1, lats)}
        down = {"lat": lax.rem(lat + lats - 1, lats)}
        narrow = kind == "s" or t == 0
        source = lat_out.at[slot] if narrow else lat_wide.at[t - 1]
        target = lat_in.at[slot] if narrow else lat_rows.at[slot]
        return (
            remote((kind + "lon", t, 0), lon_out.at[slot], lon_in.at[slot, 0], east),
            remote((kind + "lon", t, 1), lon_out.at[slot], lon_in.at[slot, 1], west),
            remote((kind + "lat", t, 0), source.at[1], target.at[0], up),
            remote((kind + "lat", t, 1), source.at[0], target.at[1], down),
        )

    def start_edges(copies):
        copies[0].start()
        copies[1].start()

        @pl.when(lat < lats - 1)
        def _():
            copies[2].start()

        @pl.when(lat > 0)
        def _():
            copies[3].start()

    def await_edges(copies, slot):
        narrow = slot == 0 or slot >= STEPS
        copies[0].wait_recv()
        copies[1].wait_recv()

        def settle(copy, side, present):
            @pl.when(present)
            def _():
                copy.wait_recv()
                if narrow:
                    lat_rows[slot, side] = lat_in[slot, side].astype(F32)

            @pl.when(jnp.logical_not(present))
            def _():
                lat_rows[slot, side] = jnp.zeros((fields * levels, lanes), F32)

        settle(copies[2], 0, lat > 0)
        settle(copies[3], 1, lat < lats - 1)

        for f in range(fields):
            lon_mix[slot, f] = jnp.where(
                lax.rem(lane, 2) == 0,
                pltpu.roll(lon_in[slot, 0, f], 1, 1),
                pltpu.roll(lon_in[slot, 1, f], lanes - 1, 1),
            )

    def await_edges_sent(copies):
        copies[0].wait_send()
        copies[1].wait_send()

        @pl.when(lat < lats - 1)
        def _():
            copies[2].wait_send()

        @pl.when(lat > 0)
        def _():
            copies[3].wait_send()

    def at(f, level):
        return pl.ds(pl.multiple_of(f * per_field + level * rows, rows), rows)

    def note_edges(level, tile, packed):
        spot = 2 * level
        here = (lane == spot) | (lane == lax.rem(spot + lanes - 1, lanes))
        return jnp.where(here, pltpu.roll(tile, spot, 1), packed)

    def pack_rows(tiles_ref, target):
        for f in range(fields):
            for side in range(2):
                first = f * per_field + side * (rows - 1)
                edge = tiles_ref[pl.ds(first, levels, stride=rows), :]
                target[side, f * levels : (f + 1) * levels, :] = edge.astype(target.dtype)

    no_tiles = tuple(jnp.zeros((rows, lanes), F32) for _ in range(fields))

    def spread(load, tiles_ref, slot):
        def body(m, packed):
            done = []
            for f in range(fields):
                first = pl.multiple_of(f * per_field + m * 2 * rows, 2 * rows)
                both = load(pl.ds(first, 2 * rows))
                tiles_ref[pl.ds(first, 2 * rows), :] = both
                p = packed[f]
                for i in range(2):
                    p = note_edges(2 * m + i, both[i * rows : (i + 1) * rows], p)
                done.append(p)
            return tuple(done)

        packed = lax.fori_loop(0, levels // 2, body, no_tiles, unroll=4)
        for f in range(fields):
            lon_out[slot, f] = packed[f]
        pack_rows(tiles_ref, lat_out.at[slot])

    for copy in local:
        copy.wait()
    spread(lambda where: allb[vec, where, :].astype(F32), field, 0)
    field_edges = [edge_copies("f", t, t) for t in range(STEPS)]
    state_edges = [edge_copies("s", STEPS + t, t) for t in range(STEPS)]
    start_edges(field_edges[0])

    traj_copies[0].wait_recv()
    slices = {}
    passes = {}
    for t in range(STEPS):
        sel[t] = jnp.where(
            owner_ref[t] == vec,
            own_traj[own_half, :].astype(F32),
            sib_traj[own_half, :].astype(F32),
        ).astype(BF16)
        for d in range(1, pairs):
            slices[t, d] = remote(
                ("slice", t, d), sel.at[t], rcv.at[t, d - 1, own_half], partner(d)
            )
            passes[t, d] = remote(
                ("pass", t, d), rcv.at[t, d - 1, own_half], rcv.at[t, d - 1, own_half], to_sibling
            )
            slices[t, d].start()

    def pivots(level, carry):
        done = []
        for f in range(fields):
            above, ratio = carry[f]
            below = jnp.full((rows, lanes), diff_ref[f, level], F32)
            inv = 1.0 / (1.0 + below + above - above * ratio)
            coef[0, at(f, level), :] = inv
            coef[1, at(f, level), :] = above * inv
            coef[2, at(f, level), :] = below * inv
            done.append((below, below * inv))
        return tuple(done)

    zero = jnp.zeros((rows, lanes), F32)
    carry = lax.fori_loop(0, levels - 1, pivots, tuple((zero, zero) for _ in range(fields)))
    for f in range(fields):
        above, ratio = carry[f]
        inv = 1.0 / (1.0 + above - above * ratio)
        coef[0, at(f, levels - 1), :] = inv
        coef[1, at(f, levels - 1), :] = above * inv
        coef[2, at(f, levels - 1), :] = zero

    def take_state(t):
        for d in range(1, pairs):
            slices[t, d].wait_recv()
            passes[t, d].start()

    def build_state(t):
        for d in range(1, pairs):
            passes[t, d].wait_recv()
        holder = owner_ref[t] // 2
        mine = owner_ref[t] == vec

        def load_state(where):
            block = jnp.where(
                mine, own_traj[where, :].astype(F32), sib_traj[where, :].astype(F32)
            )
            for d in range(1, pairs):
                source = lax.rem(pair + pairs - d, pairs)
                block = jnp.where(holder == source, rcv[t, d - 1, where, :].astype(F32), block)
            return block

        spread(load_state, state.at[t], STEPS + t)
        start_edges(state_edges[t])

    def dlon(tile, mix, shift):
        mix = pltpu.roll(mix, shift, 1)
        after = jnp.where(lane == lanes - 1, mix, pltpu.roll(tile, lanes - 1, 1))
        before = jnp.where(lane == 0, mix, pltpu.roll(tile, 1, 1))
        return after - before

    def dlat(tile, slot, f, level):
        low = lat_rows[slot, 0, pl.ds(f * levels + level, 1), :]
        high = lat_rows[slot, 1, pl.ds(f * levels + level, 1), :]
        after = jnp.where(row == rows - 1, high, pltpu.roll(tile, rows - 1, 0))
        before = jnp.where(row == 0, low, pltpu.roll(tile, 1, 0))
        return after - before

    def step(t):
        fslot, sslot = t, STEPS + t

        def forward(level, solved):
            tiles = [field[at(f, level), :] for f in range(fields)]
            states = [state[t, at(f, level), :] for f in range(fields)]
            wind_u, wind_v = states[:2]
            pert_u, pert_v = tiles[:2]
            shift = lax.rem(lanes - 2 * level, lanes)
            done = []
            for f in range(fields):
                a, s = tiles[f], states[f]
                change = wind_u * dlon(a, lon_mix[fslot, f], shift)
                change += wind_v * dlat(a, fslot, f, level)
                change += pert_u * dlon(s, lon_mix[sslot, f], shift)
                change += pert_v * dlat(s, sslot, f, level)
                moved = a - (0.5 * COURANT) * change
                done.append(moved * coef[0, at(f, level), :] + solved[f] * coef[1, at(f, level), :])
            for f in range(fields):
                field[at(f, level), :] = done[f]
            return tuple(done)

        lax.fori_loop(0, levels, forward, no_tiles, unroll=8)
        if t + 1 < STEPS:
            take_state(t + 1)
        last = t == STEPS - 1

        def backward(k, carry):
            level = levels - 1 - k
            above, packed = carry
            done, edges = [], []
            for f in range(fields):
                x = field[at(f, level), :] + coef[2, at(f, level), :] * above[f]
                field[at(f, level), :] = x
                done.append(x)
                if not last:
                    edges.append(note_edges(level, x, packed[f]))
            return tuple(done), tuple(edges)

        _, packed = lax.fori_loop(0, levels, backward, (no_tiles, () if last else no_tiles), unroll=8)
        if not last:
            for f in range(fields):
                lon_out[t + 1, f] = packed[f]
            pack_rows(field, lat_wide.at[t])
            start_edges(field_edges[t + 1])

    def relay_field(f):
        for d in range(1, pairs):
            cross[f, d].wait_recv()
            relay[f, d].start()

    take_state(0)
    for d in range(1, pairs):
        for f in range(1, fields):
            cross[f, d].start()
    traj_copies[1].wait_recv()
    relayed = 0
    for t in range(STEPS):
        build_state(t)
        if t == STEPS - 1:
            while relayed < fields - 1:
                relay_field(relayed)
                relayed += 1
        await_edges(field_edges[t], t)
        await_edges(state_edges[t], STEPS + t)
        step(t)
    while relayed < fields:
        relay_field(relayed)
        relayed += 1
    basis_copy.wait_recv()

    total_rows = rows * lats
    total = float(fields * levels * total_rows * lanes * lons)
    row_ids = (lat * rows + row).astype(F32)
    cosine = jnp.cos((row_ids + 0.5) * (math.pi / total_rows) - math.pi / 2)

    def load_vector(i, f, m):
        first = pl.multiple_of(f * per_field + m * 2 * rows, 2 * rows)
        return allb[i, pl.ds(first, 2 * rows), :].astype(F32)

    acc = tuple(zero for _ in range(groups))
    for f in range(fields):
        for d in range(1, pairs):
            relay[f, d].wait_recv()
        scale = weight_ref[f] * cosine / total

        def gram(m, acc):
            acc = list(acc)
            low = field[at(f, 2 * m), :] * scale
            high = field[at(f, 2 * m + 1), :] * scale
            for i in range(groups):
                b = load_vector(i, f, m)
                acc[i] += b[:rows] * low + b[rows:] * high
            return tuple(acc)

        acc = lax.fori_loop(0, levels // 2, gram, acc, unroll=8)
    part = jnp.zeros((8, lanes), F32)
    part_row = lax.broadcasted_iota(jnp.int32, (8, lanes), 0)
    for i in range(groups):
        part = jnp.where(part_row == i, jnp.sum(acc[i], axis=0, keepdims=True), part)
    sums[me] = part
    sum_copies = []
    for k in range(1, tiles):
        copy = remote(("sum", k), sums.at[me], sums.at[me], other_tile(k))
        copy.start()
        sum_copies.append(copy)
    for copy in sum_copies:
        copy.wait_recv()
    whole = sums[0]
    for k in range(1, tiles):
        whole += sums[k]
    column = jnp.sum(whole, axis=1, keepdims=True)
    cols[vec] = jnp.broadcast_to(column, (8, lanes))
    col_copies = []
    for k in range(1, groups):
        copy = remote(("col", k), cols.at[vec], cols.at[vec], other_vec(k))
        copy.start()
        col_copies.append(copy)
    factor = [jnp.broadcast_to(column[i : i + 1], (rows, lanes)) for i in range(groups)]

    def residual(m, carry):
        for f in range(fields):
            low, high = field[at(f, 2 * m), :], field[at(f, 2 * m + 1), :]
            for i in range(groups):
                b = load_vector(i, f, m)
                low -= b[:rows] * factor[i]
                high -= b[rows:] * factor[i]
            out_ref[f, 2 * m] = low
            out_ref[f, 2 * m + 1] = high
        return carry

    lax.fori_loop(0, levels // 2, residual, 0, unroll=4)
    for copy in col_copies:
        copy.wait_recv()
    table = jnp.zeros((8, lanes), F32)
    wide_lane = lax.broadcasted_iota(jnp.int32, (8, lanes), 1)
    for j in range(groups):
        table = jnp.where(wide_lane == j, cols[j], table)
    coup_ref[...] = table[:groups, :groups]

    for copy in traj_copies:
        copy.wait_send()
    basis_copy.wait_send()
    for d in range(1, pairs):
        for f in range(fields):
            cross[f, d].wait_send()
            relay[f, d].wait_send()
        for t in range(STEPS):
            slices[t, d].wait_send()
            passes[t, d].wait_send()
    for t in range(STEPS):
        await_edges_sent(field_edges[t])
        await_edges_sent(state_edges[t])
    for copy in sum_copies + col_copies:
        copy.wait_send()


def solution(mesh):
    groups, lats, lons = mesh.shape["vec"], mesh.shape["lat"], mesh.shape["lon"]

    def per_device(basis, trajectory, slice_owner, diffusion, energy_weight):
        _, fields, levels, rows, lanes = basis.shape
        size = fields * levels * rows
        pairs, tiles = groups // 2, lats * lons
        ids = copy_names(pairs, tiles, groups, fields)
        slots = 2 * STEPS
        vmem = pl.BlockSpec(memory_space=pltpu.VMEM)
        hbm = pl.BlockSpec(memory_space=pltpu.HBM)
        residual_block, coupling = pl.pallas_call(
            functools.partial(kernel, (fields, levels, rows, lanes), (groups, lats, lons), ids),
            out_shape=(
                jax.ShapeDtypeStruct((fields, levels, rows, lanes), F32),
                jax.ShapeDtypeStruct((groups, groups), F32),
            ),
            in_specs=[hbm] * 5,
            out_specs=(vmem, vmem),
            scratch_shapes=[
                pltpu.SMEM(slice_owner.shape, jnp.int32),
                pltpu.SMEM(diffusion.shape, F32),
                pltpu.SMEM(energy_weight.shape, F32),
                pltpu.VMEM((size, lanes), BF16),
                pltpu.VMEM((size, lanes), BF16),
                pltpu.VMEM((STEPS, size // 2, lanes), BF16),
                pltpu.VMEM((STEPS, max(pairs - 1, 1), size, lanes), BF16),
                pltpu.VMEM((groups, size, lanes), BF16),
                pltpu.VMEM((size, lanes), F32),
                pltpu.VMEM((STEPS, size, lanes), F32),
                pltpu.VMEM((3, size, lanes), F32),
                pltpu.VMEM((slots, fields, rows, lanes), F32),
                pltpu.VMEM((slots, 2, fields, rows, lanes), F32),
                pltpu.VMEM((slots, 2, fields * levels, lanes), BF16),
                pltpu.VMEM((slots, 2, fields * levels, lanes), BF16),
                pltpu.VMEM((STEPS - 1, 2, fields * levels, lanes), F32),
                pltpu.VMEM((slots, fields, rows, lanes), F32),
                pltpu.VMEM((slots, 2, fields * levels, lanes), F32),
                pltpu.VMEM((tiles, 8, lanes), F32),
                pltpu.VMEM((groups, 8, lanes), F32),
                pltpu.SemaphoreType.DMA((5,)),
                pltpu.SemaphoreType.DMA((len(ids),)),
                pltpu.SemaphoreType.DMA((len(ids),)),
            ],
            compiler_params=pltpu.CompilerParams(
                collective_id=0, has_side_effects=True, vmem_limit_bytes=48 * 1024 * 1024
            ),
        )(
            basis.reshape(size, lanes),
            trajectory.reshape(size, lanes),
            slice_owner,
            diffusion,
            energy_weight,
        )
        return residual_block[None], coupling

    return jax.shard_map(
        per_device,
        mesh=mesh,
        in_specs=(
            P("vec", None, None, "lat", "lon"),
            P("vec", None, None, "lat", "lon"),
            P(),
            P(),
            P(),
        ),
        out_specs=(P("vec", None, None, "lat", "lon"), P()),
        check_vma=False,
    )
```

time: 59.9 us -> 46.5 us (0.78)
  Pallas kernels: 54.1 us -> 40.7 us
    pallas_call x1, Pallas kernels: 54.1 us -> 40.7 us  [per_device(): pl.pallas_call(functools.partial(kernel, (fields, levels, rows, lanes), (...]
where the time goes in v2:
time: 46.5 us; the launch traced here: 46.2 us
  Pallas kernels  40.7 us (88%)
  local copies, waits for them, and re-layouts  4.93 us (11%)
  between operations  0.66 us (1%)
    pallas_call x1, Pallas kernels, per_device(): pl.pallas_call(functools.partial(kernel, (fields, levels, rows, lanes), (...  40.7 us
    unnamed x12, local copies, waits for them, and re-layouts  4.93 us

profile of v2, /device:TPU:0, one launch (start us, length us, event | category | flops | bytes accessed | tf_op | source)
XLA Modules:
  0.0 46.2 jit_solution(15704477438592453216)
XLA Ops:
  0.6 0.0 copy-start.3
  0.6 0.0 copy-start.4
  0.7 0.6 %copy-done.3 = s32[4]{0:T(128)S(1)} copy-done((s32[4]{0:T(128)S(1)}, s32[4]{0:T(128)}, u32[]{:S(2)}) %copy-start.3) | copy-done | bytes 40
  1.3 0.0 copy-done.4
  1.3 0.0 copy-start
  1.3 1.0 %copy-done = bf16[1,5,48,8,128]{4,3,2,1,0:T(8,128)(2,1)S(1)} copy-done((bf16[1,5,48,8,128]{4,3,2,1,0:T(8,128)(2,1)S(1)}, bf16[1,5,48,8,128]{4,3,2,1,0:T(8,128)(2,1)}, u32[]{:S(2)}) %copy-start) | copy-done | bytes 491544
  2.3 0.0 copy-start.1
  2.3 1.0 %copy-done.1 = bf16[1,5,48,8,128]{4,3,2,1,0:T(8,128)(2,1)S(1)} copy-done((bf16[1,5,48,8,128]{4,3,2,1,0:T(8,128)(2,1)S(1)}, bf16[1,5,48,8,128]{4,3,2,1,0:T(8,128)(2,1)}, u32[]{:S(2)}) %copy-start.1) | copy-done | bytes 491544
  3.4 0.0 copy-start.2
  3.4 0.7 %copy-done.2 = f32[5,47]{1,0:T(8,128)S(1)} copy-done((f32[5,47]{1,0:T(8,128)S(1)}, f32[5,47]{1,0:T(8,128)}, u32[]{:S(2)}) %copy-start.2) | copy-done | bytes 964
  4.1 40.7 %shard_map.68 = (f32[5,48,8,128]{3,2,1,0:T(8,128)S(1)}, f32[4,4]{1,0:T(4,128)S(1)}) custom-call(bf16[1920,128]{1,0:T(8,128)(2,1)S(1)} %bitcast.4, bf16[1920,128]{1,0:T(8,128)(2,1)S(1)} %bitcast.5, s32[4]{0:T(128)S(1)} %copy-done.3, f32[5,47]{1,0:T(8,128)S(1)} %copy-done.2, f32[5]{0:T(128)S(1)} %copy-done.4), custom_call_target="tpu_custom_call" | custom-call | tf_op jit(solution)/shard_map/pallas_call | solution.py:501
  44.7 0.9 %copy.9 = f32[1,5,48,8,128]{4,3,2,1,0:T(8,128)} copy(f32[1,5,48,8,128]{4,3,2,1,0:T(8,128)S(1)} %bitcast.3) | data formatting | bytes 1966080
  45.7 0.6 %copy.10 = f32[4,4]{1,0:T(4,128)} copy(f32[4,4]{1,0:T(4,128)S(1)} %get-tuple-element.9) | data formatting | bytes 128
Async XLA Ops:
  0.6 0.7 %copy-start.3 = (s32[4]{0:T(128)S(1)}, s32[4]{0:T(128)}, u32[]{:S(2)}) copy-start(s32[4]{0:T(128)} %owner_in.1) | copy-start | bytes 52
  0.6 0.7 %copy-start.4 = (f32[5]{0:T(128)S(1)}, f32[5]{0:T(128)}, u32[]{:S(2)}) copy-start(f32[5]{0:T(128)} %weight_in.1) | copy-start | bytes 64
  1.3 1.0 %copy-start = (bf16[1,5,48,8,128]{4,3,2,1,0:T(8,128)(2,1)S(1)}, bf16[1,5,48,8,128]{4,3,2,1,0:T(8,128)(2,1)}, u32[]{:S(2)}) copy-start(bf16[1,5,48,8,128]{4,3,2,1,0:T(8,128)(2,1)} %param.5) | copy-start | bytes 1474564
  2.3 1.0 %copy-start.1 = (bf16[1,5,48,8,128]{4,3,2,1,0:T(8,128)(2,1)S(1)}, bf16[1,5,48,8,128]{4,3,2,1,0:T(8,128)(2,1)}, u32[]{:S(2)}) copy-start(bf16[1,5,48,8,128]{4,3,2,1,0:T(8,128)(2,1)} %param.6) | copy-start | bytes 1474564
  3.4 0.7 %copy-start.2 = (f32[5,47]{1,0:T(8,128)S(1)}, f32[5,47]{1,0:T(8,128)}, u32[]{:S(2)}) copy-start(f32[5,47]{1,0:T(8,128)} %diff_in.1) | copy-start | bytes 2824

commit v3 on v2

--- a/solution.py
+++ b/solution.py
@@ -53,7 +53,6 @@
     lon_in,
     lat_out,
     lat_in,
-    lat_wide,
     lon_mix,
     lat_rows,
     sums,
@@ -153,9 +152,7 @@
         west = {"lon": lax.rem(lon + lons - 1, lons)}
         up = {"lat": lax.rem(lat + 1, lats)}
         down = {"lat": lax.rem(lat + lats - 1, lats)}
-        narrow = kind == "s" or t == 0
-        source = lat_out.at[slot] if narrow else lat_wide.at[t - 1]
-        target = lat_in.at[slot] if narrow else lat_rows.at[slot]
+        source, target = lat_out.at[slot], lat_in.at[slot]
         return (
             remote((kind + "lon", t, 0), lon_out.at[slot], lon_in.at[slot, 0], east),
             remote((kind + "lon", t, 1), lon_out.at[slot], lon_in.at[slot, 1], west),
@@ -176,7 +173,6 @@
             copies[3].start()
 
     def await_edges(copies, slot):
-        narrow = slot == 0 or slot >= STEPS
         copies[0].wait_recv()
         copies[1].wait_recv()
 
@@ -184,8 +180,7 @@
             @pl.when(present)
             def _():
                 copy.wait_recv()
-                if narrow:
-                    lat_rows[slot, side] = lat_in[slot, side].astype(F32)
+                lat_rows[slot, side] = lat_in[slot, side].astype(F32)
 
             @pl.when(jnp.logical_not(present))
             def _():
@@ -250,11 +245,6 @@
 
     for copy in local:
         copy.wait()
-    spread(lambda where: allb[vec, where, :].astype(F32), field, 0)
-    field_edges = [edge_copies("f", t, t) for t in range(STEPS)]
-    state_edges = [edge_copies("s", STEPS + t, t) for t in range(STEPS)]
-    start_edges(field_edges[0])
-
     traj_copies[0].wait_recv()
     slices = {}
     passes = {}
@@ -271,7 +261,14 @@
             passes[t, d] = remote(
                 ("pass", t, d), rcv.at[t, d - 1, own_half], rcv.at[t, d - 1, own_half], to_sibling
             )
-            slices[t, d].start()
+        if t == 0:
+            for d in range(1, pairs):
+                slices[t, d].start()
+
+    spread(lambda where: allb[vec, where, :].astype(F32), field, 0)
+    field_edges = [edge_copies("f", t, t) for t in range(STEPS)]
+    state_edges = [edge_copies("s", STEPS + t, t) for t in range(STEPS)]
+    start_edges(field_edges[0])
 
     def pivots(level, carry):
         done = []
@@ -297,6 +294,8 @@
     def take_state(t):
         for d in range(1, pairs):
             slices[t, d].wait_recv()
+            if t + 1 < STEPS:
+                slices[t + 1, d].start()
             passes[t, d].start()
 
     def build_state(t):
@@ -373,7 +372,7 @@
         if not last:
             for f in range(fields):
                 lon_out[t + 1, f] = packed[f]
-            pack_rows(field, lat_wide.at[t])
+            pack_rows(field, lat_out.at[t + 1])
             start_edges(field_edges[t + 1])
 
     def relay_field(f):
@@ -382,13 +381,14 @@
             relay[f, d].start()
 
     take_state(0)
-    for d in range(1, pairs):
-        for f in range(1, fields):
-            cross[f, d].start()
     traj_copies[1].wait_recv()
     relayed = 0
     for t in range(STEPS):
         build_state(t)
+        if t == 0:
+            for d in range(1, pairs):
+                for f in range(1, fields):
+                    cross[f, d].start()
         if t == STEPS - 1:
             while relayed < fields - 1:
                 relay_field(relayed)
@@ -450,18 +450,25 @@
         col_copies.append(copy)
     factor = [jnp.broadcast_to(column[i : i + 1], (rows, lanes)) for i in range(groups)]
 
-    def residual(m, carry):
-        for f in range(fields):
+    out_copies = []
+    for f in range(fields):
+
+        def residual(m, carry):
             low, high = field[at(f, 2 * m), :], field[at(f, 2 * m + 1), :]
             for i in range(groups):
                 b = load_vector(i, f, m)
                 low -= b[:rows] * factor[i]
                 high -= b[rows:] * factor[i]
-            out_ref[f, 2 * m] = low
-            out_ref[f, 2 * m + 1] = high
-        return carry
-
-    lax.fori_loop(0, levels // 2, residual, 0, unroll=4)
+            field[at(f, 2 * m), :] = low
+            field[at(f, 2 * m + 1), :] = high
+            return carry
+
+        lax.fori_loop(0, levels // 2, residual, 0, unroll=8)
+        chunk = pl.ds(f * per_field, per_field)
+        copy = pltpu.make_async_copy(field.at[chunk], out_ref.at[chunk], local_sem.at[5 + f])
+        copy.start()
+        out_copies.append(copy)
+
     for copy in col_copies:
         copy.wait_recv()
     table = jnp.zeros((8, lanes), F32)
@@ -470,6 +477,8 @@
         table = jnp.where(wide_lane == j, cols[j], table)
     coup_ref[...] = table[:groups, :groups]
 
+    for copy in out_copies:
+        copy.wait()
     for copy in traj_copies:
         copy.wait_send()
     basis_copy.wait_send()
@@ -501,11 +510,11 @@
         residual_block, coupling = pl.pallas_call(
             functools.partial(kernel, (fields, levels, rows, lanes), (groups, lats, lons), ids),
             out_shape=(
-                jax.ShapeDtypeStruct((fields, levels, rows, lanes), F32),
+                jax.ShapeDtypeStruct((size, lanes), F32),
                 jax.ShapeDtypeStruct((groups, groups), F32),
             ),
             in_specs=[hbm] * 5,
-            out_specs=(vmem, vmem),
+            out_specs=(hbm, vmem),
             scratch_shapes=[
                 pltpu.SMEM(slice_owner.shape, jnp.int32),
                 pltpu.SMEM(diffusion.shape, F32),
@@ -522,17 +531,16 @@
                 pltpu.VMEM((slots, 2, fields, rows, lanes), F32),
                 pltpu.VMEM((slots, 2, fields * levels, lanes), BF16),
                 pltpu.VMEM((slots, 2, fields * levels, lanes), BF16),
-                pltpu.VMEM((STEPS - 1, 2, fields * levels, lanes), F32),
                 pltpu.VMEM((slots, fields, rows, lanes), F32),
                 pltpu.VMEM((slots, 2, fields * levels, lanes), F32),
                 pltpu.VMEM((tiles, 8, lanes), F32),
                 pltpu.VMEM((groups, 8, lanes), F32),
-                pltpu.SemaphoreType.DMA((5,)),
+                pltpu.SemaphoreType.DMA((5 + fields,)),
                 pltpu.SemaphoreType.DMA((len(ids),)),
                 pltpu.SemaphoreType.DMA((len(ids),)),
             ],
             compiler_params=pltpu.CompilerParams(
-                collective_id=0, has_side_effects=True, vmem_limit_bytes=48 * 1024 * 1024
+                collective_id=0, has_side_effects=True, vmem_limit_bytes=60 * 1024 * 1024
             ),
         )(
             basis.reshape(size, lanes),
@@ -541,7 +549,7 @@
             diffusion,
             energy_weight,
         )
-        return residual_block[None], coupling
+        return residual_block.reshape(basis.shape), coupling
 
     return jax.shard_map(
         per_device,

time: 46.5 us -> 44 us (0.946)
  local copies, waits for them, and re-layouts: 4.93 us -> 2.79 us
    unnamed x12 -> x4, local copies, waits for them, and re-layouts: 4.93 us -> 2.79 us
where the time goes in v3:
time: 44 us; the launch traced here: 43.9 us
  Pallas kernels  40.4 us (92%)
  local copies, waits for them, and re-layouts  2.79 us (6%)
  between operations  0.65 us (1%)
    pallas_call x1, Pallas kernels, per_device(): pl.pallas_call(functools.partial(kernel, (fields, levels, rows, lanes), (...  40.4 us
    unnamed x4, local copies, waits for them, and re-layouts  2.79 us

profile of v3, /device:TPU:0, one launch (start us, length us, event | category | flops | bytes accessed | tf_op | source)
XLA Modules:
  0.0 43.9 jit_solution(6437455884271013634)
XLA Ops:
  0.6 40.4 %shard_map.68 = (f32[1920,128]{1,0:T(8,128)}, f32[4,4]{1,0:T(4,128)}) custom-call(bf16[1920,128]{1,0:T(8,128)(2,1)} %bitcast.4, bf16[1920,128]{1,0:T(8,128)(2,1)} %bitcast.5, s32[4]{0:T(128)} %owner_in.1, f32[5,47]{1,0:T(8,128)} %diff_in.1, f32[5]{0:T(128)} %weight_in.1), custom_call_target="tpu_custom_call" | custom-call | tf_op jit(solution)/shard_map/pallas_call | solution.py:510
  41.1 0.0 copy-start
  41.1 2.2 %copy.9 = f32[1,5,48,8,128]{4,3,2,1,0:T(8,128)} copy(f32[1,5,48,8,128]{4,3,2,1,0:T(8,128)} %bitcast.3) | data formatting | bytes 1966080
  43.3 0.0 copy-done
  43.3 0.6 %copy.10 = f32[4,4]{1,0:T(4,128)} copy(f32[4,4]{1,0:T(4,128)S(1)} %copy-done) | data formatting | bytes 128
Async XLA Ops:
  41.1 2.2 %copy-start = (f32[4,4]{1,0:T(4,128)S(1)}, f32[4,4]{1,0:T(4,128)}, u32[]{:S(2)}) copy-start(f32[4,4]{1,0:T(4,128)} %get-tuple-element.9) | copy-start | bytes 196

commit v4 on v3

--- a/solution.py
+++ b/solution.py
@@ -9,6 +9,8 @@
 from jax.sharding import PartitionSpec as P
 
 STEPS = 2
+PIECES = 2
+CHUNKS = 4
 COURANT = 0.25
 MESH = pl.DeviceIdType.MESH
 F32 = jnp.float32
@@ -19,7 +21,9 @@
     names = [("traj", 0), ("traj", 1), "basis"]
     for d in range(1, pairs):
         names += [(kind, k, d) for kind in ("cross", "relay") for k in range(fields)]
-        names += [(kind, t, d) for kind in ("slice", "pass") for t in range(STEPS)]
+        names += [
+            (kind, t, d, i) for kind in ("slice", "pass") for t in range(STEPS) for i in range(PIECES)
+        ]
     for t in range(STEPS):
         names += [(kind, t, s) for kind in ("flon", "flat", "slon", "slat") for s in range(2)]
     names += [("sum", k) for k in range(1, tiles)]
@@ -48,6 +52,7 @@
     allb,
     field,
     state,
+    moved,
     coef,
     lon_out,
     lon_in,
@@ -67,6 +72,7 @@
     size = fields * levels * rows
     per_field = levels * rows
     half = size // 2
+    piece = half // PIECES
     vec = lax.axis_index("vec")
     lat = lax.axis_index("lat")
     lon = lax.axis_index("lon")
@@ -255,15 +261,15 @@
             sib_traj[own_half, :].astype(F32),
         ).astype(BF16)
         for d in range(1, pairs):
-            slices[t, d] = remote(
-                ("slice", t, d), sel.at[t], rcv.at[t, d - 1, own_half], partner(d)
-            )
-            passes[t, d] = remote(
-                ("pass", t, d), rcv.at[t, d - 1, own_half], rcv.at[t, d - 1, own_half], to_sibling
-            )
-        if t == 0:
-            for d in range(1, pairs):
-                slices[t, d].start()
+            for i in range(PIECES):
+                first = pl.multiple_of(core * half + i * piece, 16)
+                there = rcv.at[t, d - 1, pl.ds(first, piece)]
+                slices[t, d, i] = remote(
+                    ("slice", t, d, i), sel.at[t, pl.ds(i * piece, piece)], there, partner(d)
+                )
+                passes[t, d, i] = remote(("pass", t, d, i), there, there, to_sibling)
+                if t == 0:
+                    slices[t, d, i].start()
 
     spread(lambda where: allb[vec, where, :].astype(F32), field, 0)
     field_edges = [edge_copies("f", t, t) for t in range(STEPS)]
@@ -291,16 +297,19 @@
         coef[1, at(f, levels - 1), :] = above * inv
         coef[2, at(f, levels - 1), :] = zero
 
+    every = [(d, i) for i in range(PIECES) for d in range(1, pairs)]
+
     def take_state(t):
-        for d in range(1, pairs):
-            slices[t, d].wait_recv()
-            if t + 1 < STEPS:
-                slices[t + 1, d].start()
-            passes[t, d].start()
+        for d, i in every:
+            slices[t, d, i].wait_recv()
+            passes[t, d, i].start()
+        if t + 1 < STEPS:
+            for d, i in every:
+                slices[t + 1, d, i].start()
 
     def build_state(t):
-        for d in range(1, pairs):
-            passes[t, d].wait_recv()
+        for d, i in every:
+            passes[t, d, i].wait_recv()
         holder = owner_ref[t] // 2
         mine = owner_ref[t] == vec
 
@@ -316,37 +325,59 @@
         spread(load_state, state.at[t], STEPS + t)
         start_edges(state_edges[t])
 
-    def dlon(tile, mix, shift):
-        mix = pltpu.roll(mix, shift, 1)
-        after = jnp.where(lane == lanes - 1, mix, pltpu.roll(tile, lanes - 1, 1))
-        before = jnp.where(lane == 0, mix, pltpu.roll(tile, 1, 1))
-        return after - before
-
-    def dlat(tile, slot, f, level):
-        low = lat_rows[slot, 0, pl.ds(f * levels + level, 1), :]
-        high = lat_rows[slot, 1, pl.ds(f * levels + level, 1), :]
-        after = jnp.where(row == rows - 1, high, pltpu.roll(tile, rows - 1, 0))
-        before = jnp.where(row == 0, low, pltpu.roll(tile, 1, 0))
-        return after - before
+    def dlon(tile):
+        after = jnp.where(lane == lanes - 1, 0.0, pltpu.roll(tile, lanes - 1, 1))
+        return after - jnp.where(lane == 0, 0.0, pltpu.roll(tile, 1, 1))
+
+    def dlat(tile):
+        after = jnp.where(row == rows - 1, 0.0, pltpu.roll(tile, rows - 1, 0))
+        return after - jnp.where(row == 0, 0.0, pltpu.roll(tile, 1, 0))
+
+    lon_sign = jnp.where(lane == lanes - 1, 1.0, jnp.where(lane == 0, -1.0, 0.0))
+    lat_sign = jnp.where(row == rows - 1, 1.0, jnp.where(row == 0, -1.0, 0.0))
+    weight = 0.5 * COURANT
+
+    def interior(t):
+        def body(level, carry):
+            tiles = [field[at(f, level), :] for f in range(fields)]
+            states = [state[t, at(f, level), :] for f in range(fields)]
+            for f in range(fields):
+                change = states[0] * dlon(tiles[f]) + states[1] * dlat(tiles[f])
+                change += tiles[0] * dlon(states[f]) + tiles[1] * dlat(states[f])
+                moved[at(f, level), :] = tiles[f] - weight * change
+            return carry
+
+        lax.fori_loop(0, levels, body, 0, unroll=4)
+
+    def beyond(slot, f, level):
+        place = pl.ds(f * levels + level, 1)
+        return jnp.where(row == 0, lat_rows[slot, 0, place, :], lat_rows[slot, 1, place, :])
+
+    relayed = []
+
+    def relay_until(end):
+        for f in range(len(relayed), end):
+            for d in range(1, pairs):
+                cross[f, d].wait_recv()
+                relay[f, d].start()
+            relayed.append(f)
 
     def step(t):
         fslot, sslot = t, STEPS + t
 
         def forward(level, solved):
-            tiles = [field[at(f, level), :] for f in range(fields)]
-            states = [state[t, at(f, level), :] for f in range(fields)]
-            wind_u, wind_v = states[:2]
-            pert_u, pert_v = tiles[:2]
             shift = lax.rem(lanes - 2 * level, lanes)
+            wind_u = state[t, at(0, level), :] * (weight * lon_sign)
+            wind_v = state[t, at(1, level), :] * (weight * lat_sign)
+            pert_u = field[at(0, level), :] * (weight * lon_sign)
+            pert_v = field[at(1, level), :] * (weight * lat_sign)
             done = []
             for f in range(fields):
-                a, s = tiles[f], states[f]
-                change = wind_u * dlon(a, lon_mix[fslot, f], shift)
-                change += wind_v * dlat(a, fslot, f, level)
-                change += pert_u * dlon(s, lon_mix[sslot, f], shift)
-                change += pert_v * dlat(s, sslot, f, level)
-                moved = a - (0.5 * COURANT) * change
-                done.append(moved * coef[0, at(f, level), :] + solved[f] * coef[1, at(f, level), :])
+                change = wind_u * pltpu.roll(lon_mix[fslot, f], shift, 1)
+                change += pert_u * pltpu.roll(lon_mix[sslot, f], shift, 1)
+                change += wind_v * beyond(fslot, f, level) + pert_v * beyond(sslot, f, level)
+                all_moved = moved[at(f, level), :] - change
+                done.append(all_moved * coef[0, at(f, level), :] + solved[f] * coef[1, at(f, level), :])
             for f in range(fields):
                 field[at(f, level), :] = done[f]
             return tuple(done)
@@ -355,6 +386,8 @@
         if t + 1 < STEPS:
             take_state(t + 1)
         last = t == STEPS - 1
+        if last:
+            relay_until(fields - 2)
 
         def backward(k, carry):
             level = levels - 1 - k
@@ -375,30 +408,21 @@
             pack_rows(field, lat_out.at[t + 1])
             start_edges(field_edges[t + 1])
 
-    def relay_field(f):
-        for d in range(1, pairs):
-            cross[f, d].wait_recv()
-            relay[f, d].start()
-
     take_state(0)
     traj_copies[1].wait_recv()
-    relayed = 0
     for t in range(STEPS):
         build_state(t)
         if t == 0:
             for d in range(1, pairs):
                 for f in range(1, fields):
                     cross[f, d].start()
+        interior(t)
         if t == STEPS - 1:
-            while relayed < fields - 1:
-                relay_field(relayed)
-                relayed += 1
+            relay_until(min(2, fields))
         await_edges(field_edges[t], t)
         await_edges(state_edges[t], STEPS + t)
         step(t)
-    while relayed < fields:
-        relay_field(relayed)
-        relayed += 1
+    relay_until(fields)
     basis_copy.wait_recv()
 
     total_rows = rows * lats
@@ -487,13 +511,28 @@
             cross[f, d].wait_send()
             relay[f, d].wait_send()
         for t in range(STEPS):
-            slices[t, d].wait_send()
-            passes[t, d].wait_send()
+            for i in range(PIECES):
+                slices[t, d, i].wait_send()
+                passes[t, d, i].wait_send()
     for t in range(STEPS):
         await_edges_sent(field_edges[t])
         await_edges_sent(state_edges[t])
     for copy in sum_copies + col_copies:
         copy.wait_send()
+
+
+def hand_over(block_ref, coup_ref, block_out, coup_out, sem):
+    copies = [pltpu.make_async_copy(coup_ref, coup_out, sem.at[0])]
+    chunk = block_ref.shape[0] // CHUNKS
+    for i in range(CHUNKS):
+        where = pl.ds(i * chunk, chunk)
+        copies.append(
+            pltpu.make_async_copy(block_ref.at[where], block_out.at[where], sem.at[1 + i])
+        )
+    for copy in copies:
+        copy.start()
+    for copy in copies:
+        copy.wait()
 
 
 def solution(mesh):
@@ -526,6 +565,7 @@
                 pltpu.VMEM((groups, size, lanes), BF16),
                 pltpu.VMEM((size, lanes), F32),
                 pltpu.VMEM((STEPS, size, lanes), F32),
+                pltpu.VMEM((size, lanes), F32),
                 pltpu.VMEM((3, size, lanes), F32),
                 pltpu.VMEM((slots, fields, rows, lanes), F32),
                 pltpu.VMEM((slots, 2, fields, rows, lanes), F32),
@@ -549,6 +589,17 @@
             diffusion,
             energy_weight,
         )
+        residual_block, coupling = pl.pallas_call(
+            hand_over,
+            out_shape=(
+                jax.ShapeDtypeStruct((size, lanes), F32),
+                jax.ShapeDtypeStruct((groups, groups), F32),
+            ),
+            in_specs=[hbm, hbm],
+            out_specs=(hbm, hbm),
+            scratch_shapes=[pltpu.SemaphoreType.DMA((1 + CHUNKS,))],
+            compiler_params=pltpu.CompilerParams(vmem_limit_bytes=60 * 1024 * 1024),
+        )(residual_block, coupling)
         return residual_block.reshape(basis.shape), coupling
 
     return jax.shard_map(

time: 44 us -> 71.3 us (1.62)
  Pallas kernels: 40.4 us -> 70.5 us
  local copies, waits for them, and re-layouts: 2.79 us -> 0 us
    pallas_call x0 -> x1, Pallas kernels: none -> 31 us  [per_device(): pl.pallas_call(hand_over, out_shape=(jax.ShapeDtypeStruct((size, lanes),...]
    unnamed x4 -> x0, local copies, waits for them, and re-layouts: 2.79 us -> none
    pallas_call x1, Pallas kernels: 40.4 us -> 39.5 us  [per_device(): pl.pallas_call(functools.partial(kernel, (fields, levels, rows, lanes), (...]
where the time goes in v4:
time: 71.3 us; the launch traced here: 71.2 us
  Pallas kernels  70.5 us (99%)
    pallas_call x1, Pallas kernels, per_device(): pl.pallas_call(functools.partial(kernel, (fields, levels, rows, lanes), (...  39.5 us
    pallas_call x1, Pallas kernels, per_device(): pl.pallas_call(hand_over, out_shape=(jax.ShapeDtypeStruct((size, lanes),...  31 us

profile of v4, /device:TPU:0, one launch (start us, length us, event | category | flops | bytes accessed | tf_op | source)
XLA Modules:
  0.0 71.2 jit_solution(4816034746681021093)
XLA Ops:
  0.6 39.5 %shard_map.68 = (f32[1920,128]{1,0:T(8,128)}, f32[4,4]{1,0:T(4,128)}) custom-call(bf16[1920,128]{1,0:T(8,128)(2,1)} %bitcast.3, bf16[1920,128]{1,0:T(8,128)(2,1)} %bitcast.4, s32[4]{0:T(128)} %owner_in.1, f32[5,47]{1,0:T(8,128)} %diff_in.1, f32[5]{0:T(128)} %weight_in.1), custom_call_target="tpu_custom_call" | custom-call | tf_op jit(solution)/shard_map/pallas_call | solution.py:549
  40.2 31.0 %shard_map.69 = (f32[1920,128]{1,0:T(8,128)}, f32[4,4]{1,0:T(4,128)}) custom-call(f32[1920,128]{1,0:T(8,128)} %get-tuple-element.6.block_ref, f32[4,4]{1,0:T(4,128)} %get-tuple-element.7.coup_ref), custom_call_target="tpu_custom_call" | custom-call | tf_op jit(solution)/shard_map/pallas_call | solution.py:592

commit v5 on v4

--- a/solution.py
+++ b/solution.py
@@ -121,6 +121,8 @@
         pl.semaphore_signal(barrier, inc=1, device_id=other_tile(k), device_id_type=MESH)
     for k in range(1, groups):
         pl.semaphore_signal(barrier, inc=1, device_id=other_vec(k), device_id_type=MESH)
+    local[1].wait()
+    local[0].wait()
     pl.semaphore_wait(barrier, tiles + groups - 2)
 
     to_sibling = {"vec": sibling}
@@ -128,7 +130,7 @@
     far_half = pl.ds(pl.multiple_of((1 - core) * half, 16), half)
 
     traj_copies = [
-        remote(("traj", i), traj_ref.at[part], sib_traj.at[part], to_sibling)
+        remote(("traj", i), own_traj.at[part], sib_traj.at[part], to_sibling)
         for i, part in enumerate((far_half, own_half))
     ]
     traj_copies[0].start()
@@ -139,7 +141,7 @@
         for f in range(fields):
             chunk = pl.ds(f * per_field, per_field)
             cross[f, d] = remote(
-                ("cross", f, d), basis_ref.at[chunk], allb.at[vec, chunk], partner(d)
+                ("cross", f, d), allb.at[vec, chunk], allb.at[vec, chunk], partner(d)
             )
             relay[f, d] = remote(
                 ("relay", f, d), allb.at[source, chunk], allb.at[source, chunk], to_sibling
@@ -147,7 +149,7 @@
     for d in range(1, pairs):
         cross[0, d].start()
     traj_copies[1].start()
-    basis_copy = remote("basis", basis_ref, allb.at[vec], to_sibling)
+    basis_copy = remote("basis", allb.at[vec], allb.at[vec], to_sibling)
     basis_copy.start()
 
     lane = lax.broadcasted_iota(jnp.int32, (rows, lanes), 1)
@@ -249,7 +251,7 @@
             lon_out[slot, f] = packed[f]
         pack_rows(tiles_ref, lat_out.at[slot])
 
-    for copy in local:
+    for copy in local[2:]:
         copy.wait()
     traj_copies[0].wait_recv()
     slices = {}
@@ -521,17 +523,22 @@
         copy.wait_send()
 
 
-def hand_over(block_ref, coup_ref, block_out, coup_out, sem):
-    copies = [pltpu.make_async_copy(coup_ref, coup_out, sem.at[0])]
+def hand_over(block_ref, coup_ref, block_out, coup_out, block, coup, in_sem, out_sem):
     chunk = block_ref.shape[0] // CHUNKS
+    parts = [(coup_ref, coup, coup_out)]
     for i in range(CHUNKS):
         where = pl.ds(i * chunk, chunk)
-        copies.append(
-            pltpu.make_async_copy(block_ref.at[where], block_out.at[where], sem.at[1 + i])
-        )
-    for copy in copies:
+        parts.append((block_ref.at[where], block.at[where], block_out.at[where]))
+    loads, stores = [], []
+    for i, (source, here, target) in enumerate(parts):
+        loads.append(pltpu.make_async_copy(source, here, in_sem.at[i]))
+        stores.append(pltpu.make_async_copy(here, target, out_sem.at[i]))
+    for copy in loads:
         copy.start()
-    for copy in copies:
+    for load, store in zip(loads, stores):
+        load.wait()
+        store.start()
+    for copy in stores:
         copy.wait()
 
 
@@ -597,7 +604,12 @@
             ),
             in_specs=[hbm, hbm],
             out_specs=(hbm, hbm),
-            scratch_shapes=[pltpu.SemaphoreType.DMA((1 + CHUNKS,))],
+            scratch_shapes=[
+                pltpu.VMEM((size, lanes), F32),
+                pltpu.VMEM((groups, groups), F32),
+                pltpu.SemaphoreType.DMA((1 + CHUNKS,)),
+                pltpu.SemaphoreType.DMA((1 + CHUNKS,)),
+            ],
             compiler_params=pltpu.CompilerParams(vmem_limit_bytes=60 * 1024 * 1024),
         )(residual_block, coupling)
         return residual_block.reshape(basis.shape), coupling

time: 71.3 us -> 42.2 us (0.59)
  Pallas kernels: 70.5 us -> 41.4 us
    pallas_call x1, Pallas kernels: 31 us -> 2.09 us  [per_device(): pl.pallas_call(hand_over, out_shape=(jax.ShapeDtypeStruct((size, lanes),...]
where the time goes in v5:
time: 42.2 us; the launch traced here: 42.1 us
  Pallas kernels  41.4 us (98%)
  between operations  0.64 us (2%)
    pallas_call x1, Pallas kernels, per_device(): pl.pallas_call(functools.partial(kernel, (fields, levels, rows, lanes), (...  39.3 us
    pallas_call x1, Pallas kernels, per_device(): pl.pallas_call(hand_over, out_shape=(jax.ShapeDtypeStruct((size, lanes),...  2.09 us

profile of v5, /device:TPU:0, one launch (start us, length us, event | category | flops | bytes accessed | tf_op | source)
XLA Modules:
  0.0 42.1 jit_solution(17017994523005181858)
XLA Ops:
  0.6 39.3 %shard_map.68 = (f32[1920,128]{1,0:T(8,128)}, f32[4,4]{1,0:T(4,128)}) custom-call(bf16[1920,128]{1,0:T(8,128)(2,1)} %bitcast.3, bf16[1920,128]{1,0:T(8,128)(2,1)} %bitcast.4, s32[4]{0:T(128)} %owner_in.1, f32[5,47]{1,0:T(8,128)} %diff_in.1, f32[5]{0:T(128)} %weight_in.1), custom_call_target="tpu_custom_call" | custom-call | tf_op jit(solution)/shard_map/pallas_call | solution.py:556
  40.0 2.1 %shard_map.69 = (f32[1920,128]{1,0:T(8,128)}, f32[4,4]{1,0:T(4,128)}) custom-call(f32[1920,128]{1,0:T(8,128)} %get-tuple-element.6.block_ref, f32[4,4]{1,0:T(4,128)} %get-tuple-element.7.coup_ref), custom_call_target="tpu_custom_call" | custom-call | tf_op jit(solution)/shard_map/pallas_call | solution.py:599

commit v6 on v5

--- a/solution.py
+++ b/solution.py
@@ -10,7 +10,7 @@
 
 STEPS = 2
 PIECES = 2
-CHUNKS = 4
+SPLIT = 2
 COURANT = 0.25
 MESH = pl.DeviceIdType.MESH
 F32 = jnp.float32
@@ -20,7 +20,7 @@
 def copy_names(pairs, tiles, groups, fields):
     names = [("traj", 0), ("traj", 1), "basis"]
     for d in range(1, pairs):
-        names += [(kind, k, d) for kind in ("cross", "relay") for k in range(fields)]
+        names += [(kind, k, d) for kind in ("cross", "relay") for k in range(SPLIT * fields)]
         names += [
             (kind, t, d, i) for kind in ("slice", "pass") for t in range(STEPS) for i in range(PIECES)
         ]
@@ -40,7 +40,9 @@
     owner_in,
     diff_in,
     weight_in,
-    out_ref,
+    field_out,
+    allb_out,
+    column_out,
     coup_ref,
     owner_ref,
     diff_ref,
@@ -73,6 +75,8 @@
     per_field = levels * rows
     half = size // 2
     piece = half // PIECES
+    chunks = SPLIT * fields
+    chunk = per_field // SPLIT
     vec = lax.axis_index("vec")
     lat = lax.axis_index("lat")
     lon = lax.axis_index("lon")
@@ -138,16 +142,31 @@
     relay = {}
     for d in range(1, pairs):
         source = 2 * lax.rem(pair + pairs - d, pairs) + core
-        for f in range(fields):
-            chunk = pl.ds(f * per_field, per_field)
-            cross[f, d] = remote(
-                ("cross", f, d), allb.at[vec, chunk], allb.at[vec, chunk], partner(d)
+        for k in range(chunks):
+            part = pl.ds(k * chunk, chunk)
+            cross[k, d] = remote(
+                ("cross", k, d), allb.at[vec, part], allb.at[vec, part], partner(d)
             )
-            relay[f, d] = remote(
-                ("relay", f, d), allb.at[source, chunk], allb.at[source, chunk], to_sibling
+            relay[k, d] = remote(
+                ("relay", k, d), allb.at[source, part], allb.at[source, part], to_sibling
             )
-    for d in range(1, pairs):
-        cross[0, d].start()
+    sent, relayed = [], []
+
+    def send_until(end):
+        for k in range(len(sent), min(end, chunks)):
+            for d in range(1, pairs):
+                cross[k, d].start()
+            sent.append(k)
+
+    def relay_until(end):
+        for k in range(len(relayed), min(end, chunks)):
+            for d in range(1, pairs):
+                cross[k, d].wait_recv()
+                relay[k, d].start()
+            relayed.append(k)
+            send_until(len(sent) + 1)
+
+    send_until(SPLIT)
     traj_copies[1].start()
     basis_copy = remote("basis", allb.at[vec], allb.at[vec], to_sibling)
     basis_copy.start()
@@ -305,8 +324,7 @@
         for d, i in every:
             slices[t, d, i].wait_recv()
             passes[t, d, i].start()
-        if t + 1 < STEPS:
-            for d, i in every:
+            if t + 1 < STEPS:
                 slices[t + 1, d, i].start()
 
     def build_state(t):
@@ -354,15 +372,6 @@
     def beyond(slot, f, level):
         place = pl.ds(f * levels + level, 1)
         return jnp.where(row == 0, lat_rows[slot, 0, place, :], lat_rows[slot, 1, place, :])
-
-    relayed = []
-
-    def relay_until(end):
-        for f in range(len(relayed), end):
-            for d in range(1, pairs):
-                cross[f, d].wait_recv()
-                relay[f, d].start()
-            relayed.append(f)
 
     def step(t):
         fslot, sslot = t, STEPS + t
@@ -387,9 +396,10 @@
         lax.fori_loop(0, levels, forward, no_tiles, unroll=8)
         if t + 1 < STEPS:
             take_state(t + 1)
+            relay_until(SPLIT)
         last = t == STEPS - 1
         if last:
-            relay_until(fields - 2)
+            relay_until(2 * SPLIT + 1)
 
         def backward(k, carry):
             level = levels - 1 - k
@@ -415,16 +425,15 @@
     for t in range(STEPS):
         build_state(t)
         if t == 0:
-            for d in range(1, pairs):
-                for f in range(1, fields):
-                    cross[f, d].start()
+            send_until(2 * SPLIT)
         interior(t)
         if t == STEPS - 1:
-            relay_until(min(2, fields))
+            relay_until(2 * SPLIT)
         await_edges(field_edges[t], t)
         await_edges(state_edges[t], STEPS + t)
         step(t)
-    relay_until(fields)
+    field_copy = pltpu.make_async_copy(field, field_out, local_sem.at[5])
+    field_copy.start()
     basis_copy.wait_recv()
 
     total_rows = rows * lats
@@ -432,26 +441,30 @@
     row_ids = (lat * rows + row).astype(F32)
     cosine = jnp.cos((row_ids + 0.5) * (math.pi / total_rows) - math.pi / 2)
 
-    def load_vector(i, f, m):
-        first = pl.multiple_of(f * per_field + m * 2 * rows, 2 * rows)
-        return allb[i, pl.ds(first, 2 * rows), :].astype(F32)
-
     acc = tuple(zero for _ in range(groups))
-    for f in range(fields):
+    base_copies = []
+    for k in range(chunks):
+        relay_until(k + 2)
         for d in range(1, pairs):
-            relay[f, d].wait_recv()
-        scale = weight_ref[f] * cosine / total
+            relay[k, d].wait_recv()
+        scale = weight_ref[k // SPLIT] * cosine / total
+        part = pl.ds(k * chunk, chunk)
+        copy = pltpu.make_async_copy(allb.at[:, part], allb_out.at[:, part], local_sem.at[6 + k])
+        copy.start()
+        base_copies.append(copy)
 
         def gram(m, acc):
             acc = list(acc)
-            low = field[at(f, 2 * m), :] * scale
-            high = field[at(f, 2 * m + 1), :] * scale
+            first = pl.multiple_of(k * chunk + m * 2 * rows, 2 * rows)
+            both = pl.ds(first, 2 * rows)
+            weighted = field[both, :]
+            low, high = weighted[:rows] * scale, weighted[rows:] * scale
             for i in range(groups):
-                b = load_vector(i, f, m)
+                b = allb[i, both, :].astype(F32)
                 acc[i] += b[:rows] * low + b[rows:] * high
             return tuple(acc)
 
-        acc = lax.fori_loop(0, levels // 2, gram, acc, unroll=8)
+        acc = lax.fori_loop(0, chunk // (2 * rows), gram, acc, unroll=6)
     part = jnp.zeros((8, lanes), F32)
     part_row = lax.broadcasted_iota(jnp.int32, (8, lanes), 0)
     for i in range(groups):
@@ -474,27 +487,7 @@
         copy = remote(("col", k), cols.at[vec], cols.at[vec], other_vec(k))
         copy.start()
         col_copies.append(copy)
-    factor = [jnp.broadcast_to(column[i : i + 1], (rows, lanes)) for i in range(groups)]
-
-    out_copies = []
-    for f in range(fields):
-
-        def residual(m, carry):
-            low, high = field[at(f, 2 * m), :], field[at(f, 2 * m + 1), :]
-            for i in range(groups):
-                b = load_vector(i, f, m)
-                low -= b[:rows] * factor[i]
-                high -= b[rows:] * factor[i]
-            field[at(f, 2 * m), :] = low
-            field[at(f, 2 * m + 1), :] = high
-            return carry
-
-        lax.fori_loop(0, levels // 2, residual, 0, unroll=8)
-        chunk = pl.ds(f * per_field, per_field)
-        copy = pltpu.make_async_copy(field.at[chunk], out_ref.at[chunk], local_sem.at[5 + f])
-        copy.start()
-        out_copies.append(copy)
-
+    column_out[...] = jnp.broadcast_to(column, (8, lanes))
     for copy in col_copies:
         copy.wait_recv()
     table = jnp.zeros((8, lanes), F32)
@@ -503,15 +496,16 @@
         table = jnp.where(wide_lane == j, cols[j], table)
     coup_ref[...] = table[:groups, :groups]
 
-    for copy in out_copies:
+    field_copy.wait()
+    for copy in base_copies:
         copy.wait()
     for copy in traj_copies:
         copy.wait_send()
     basis_copy.wait_send()
     for d in range(1, pairs):
-        for f in range(fields):
-            cross[f, d].wait_send()
-            relay[f, d].wait_send()
+        for k in range(chunks):
+            cross[k, d].wait_send()
+            relay[k, d].wait_send()
         for t in range(STEPS):
             for i in range(PIECES):
                 slices[t, d, i].wait_send()
@@ -523,23 +517,61 @@
         copy.wait_send()
 
 
-def hand_over(block_ref, coup_ref, block_out, coup_out, block, coup, in_sem, out_sem):
-    chunk = block_ref.shape[0] // CHUNKS
-    parts = [(coup_ref, coup, coup_out)]
-    for i in range(CHUNKS):
-        where = pl.ds(i * chunk, chunk)
-        parts.append((block_ref.at[where], block.at[where], block_out.at[where]))
+def residual_kernel(
+    shape,
+    column_ref,
+    field_ref,
+    allb_ref,
+    coup_ref,
+    out_ref,
+    coup_out,
+    field,
+    allb,
+    coup,
+    load_sem,
+    store_sem,
+):
+    fields, levels, rows, lanes = shape
+    per_field = levels * rows
+    groups = allb_ref.shape[0]
     loads, stores = [], []
-    for i, (source, here, target) in enumerate(parts):
-        loads.append(pltpu.make_async_copy(source, here, in_sem.at[i]))
-        stores.append(pltpu.make_async_copy(here, target, out_sem.at[i]))
-    for copy in loads:
-        copy.start()
-    for load, store in zip(loads, stores):
-        load.wait()
-        store.start()
-    for copy in stores:
-        copy.wait()
+    for f in range(fields):
+        part = pl.ds(f * per_field, per_field)
+        loads.append(
+            (
+                pltpu.make_async_copy(field_ref.at[part], field.at[part], load_sem.at[2 * f]),
+                pltpu.make_async_copy(
+                    allb_ref.at[:, part], allb.at[:, part], load_sem.at[2 * f + 1]
+                ),
+            )
+        )
+        stores.append(pltpu.make_async_copy(field.at[part], out_ref.at[part], store_sem.at[f]))
+    coup_load = pltpu.make_async_copy(coup_ref, coup, load_sem.at[2 * fields])
+    coup_store = pltpu.make_async_copy(coup, coup_out, store_sem.at[fields])
+    for pair in loads:
+        pair[0].start()
+        pair[1].start()
+    coup_load.start()
+    factor = [jnp.broadcast_to(column_ref[i : i + 1, :], (2 * rows, lanes)) for i in range(groups)]
+    coup_load.wait()
+    coup_store.start()
+    for f in range(fields):
+        loads[f][0].wait()
+        loads[f][1].wait()
+
+        def body(m, carry):
+            both = pl.ds(pl.multiple_of(f * per_field + m * 2 * rows, 2 * rows), 2 * rows)
+            rest = field[both, :]
+            for i in range(groups):
+                rest -= allb[i, both, :].astype(F32) * factor[i]
+            field[both, :] = rest
+            return carry
+
+        lax.fori_loop(0, levels // 2, body, 0, unroll=8)
+        stores[f].start()
+    for store in stores:
+        store.wait()
+    coup_store.wait()
 
 
 def solution(mesh):
@@ -553,14 +585,16 @@
         slots = 2 * STEPS
         vmem = pl.BlockSpec(memory_space=pltpu.VMEM)
         hbm = pl.BlockSpec(memory_space=pltpu.HBM)
-        residual_block, coupling = pl.pallas_call(
+        field, all_basis, column, coupling = pl.pallas_call(
             functools.partial(kernel, (fields, levels, rows, lanes), (groups, lats, lons), ids),
             out_shape=(
                 jax.ShapeDtypeStruct((size, lanes), F32),
+                jax.ShapeDtypeStruct((groups, size, lanes), BF16),
+                jax.ShapeDtypeStruct((8, lanes), F32),
                 jax.ShapeDtypeStruct((groups, groups), F32),
             ),
             in_specs=[hbm] * 5,
-            out_specs=(hbm, vmem),
+            out_specs=(hbm, hbm, vmem, vmem),
             scratch_shapes=[
                 pltpu.SMEM(slice_owner.shape, jnp.int32),
                 pltpu.SMEM(diffusion.shape, F32),
@@ -582,7 +616,7 @@
                 pltpu.VMEM((slots, 2, fields * levels, lanes), F32),
                 pltpu.VMEM((tiles, 8, lanes), F32),
                 pltpu.VMEM((groups, 8, lanes), F32),
-                pltpu.SemaphoreType.DMA((5 + fields,)),
+                pltpu.SemaphoreType.DMA((6 + SPLIT * fields,)),
                 pltpu.SemaphoreType.DMA((len(ids),)),
                 pltpu.SemaphoreType.DMA((len(ids),)),
             ],
@@ -597,21 +631,22 @@
             energy_weight,
         )
         residual_block, coupling = pl.pallas_call(
-            hand_over,
+            functools.partial(residual_kernel, (fields, levels, rows, lanes)),
             out_shape=(
                 jax.ShapeDtypeStruct((size, lanes), F32),
                 jax.ShapeDtypeStruct((groups, groups), F32),
             ),
-            in_specs=[hbm, hbm],
+            in_specs=[vmem, hbm, hbm, hbm],
             out_specs=(hbm, hbm),
             scratch_shapes=[
                 pltpu.VMEM((size, lanes), F32),
+                pltpu.VMEM((groups, size, lanes), BF16),
                 pltpu.VMEM((groups, groups), F32),
-                pltpu.SemaphoreType.DMA((1 + CHUNKS,)),
-                pltpu.SemaphoreType.DMA((1 + CHUNKS,)),
+                pltpu.SemaphoreType.DMA((2 * fields + 1,)),
+                pltpu.SemaphoreType.DMA((fields + 1,)),
             ],
             compiler_params=pltpu.CompilerParams(vmem_limit_bytes=60 * 1024 * 1024),
-        )(residual_block, coupling)
+        )(column, field, all_basis, coupling)
         return residual_block.reshape(basis.shape), coupling
 
     return jax.shard_map(

time: 42.2 us -> 45.7 us (1.083)
  Pallas kernels: 41.4 us -> 44.9 us
    pallas_call x1, Pallas kernels: 39.3 us -> 41.3 us  [per_device(): pl.pallas_call(functools.partial(kernel, (fields, levels, rows, lanes), (...]
    pallas_call x1, Pallas kernels: 2.09 us -> 3.6 us  [per_device(): pl.pallas_call(functools.partial(residual_kernel, (fields, levels, rows,...]
where the time goes in v6:
time: 45.7 us; the launch traced here: 45.5 us
  Pallas kernels  44.9 us (98%)
  between operations  0.64 us (1%)
    pallas_call x1, Pallas kernels, per_device(): pl.pallas_call(functools.partial(kernel, (fields, levels, rows, lanes), (...  41.3 us
    pallas_call x1, Pallas kernels, per_device(): pl.pallas_call(functools.partial(residual_kernel, (fields, levels, rows,...  3.6 us

profile of v6, /device:TPU:0, one launch (start us, length us, event | category | flops | bytes accessed | tf_op | source)
XLA Modules:
  0.0 45.5 jit_solution(16415237820283289808)
XLA Ops:
  0.6 41.3 %shard_map.68 = (f32[1920,128]{1,0:T(8,128)}, bf16[4,1920,128]{2,1,0:T(8,128)(2,1)}, f32[8,128]{1,0:T(8,128)}, f32[4,4]{1,0:T(4,128)}) custom-call(bf16[1920,128]{1,0:T(8,128)(2,1)} %bitcast.3, bf16[1920,128]{1,0:T(8,128)(2,1)} %bitcast.4, s32[4]{0:T(128)} %owner_in.1, f32[5,47]{1,0:T(8,128)} %diff_in.1, f32[5]{0:T(128)} %weight_in.1), custom_call_target="tpu_custom_call" | custom-call | tf_op jit(solution)/shard_map/pallas_call | solution.py:588
  41.9 3.6 %shard_map.69 = (f32[1920,128]{1,0:T(8,128)}, f32[4,4]{1,0:T(4,128)}) custom-call(f32[8,128]{1,0:T(8,128)} %get-tuple-element.8.column_ref, f32[1920,128]{1,0:T(8,128)} %get-tuple-element.9.field_ref, bf16[4,1920,128]{2,1,0:T(8,128)(2,1)} %get-tuple-element.10.allb_ref, f32[4,4]{1,0:T(4,128)} %get-tuple-element.11.coup_ref), custom_call_target="tpu_custom_call" | custom-call | tf_op jit(solution)/shard_map/pallas_call | solution.py:633

commit v7 on v5

--- a/solution.py
+++ b/solution.py
@@ -150,7 +150,6 @@
         cross[0, d].start()
     traj_copies[1].start()
     basis_copy = remote("basis", allb.at[vec], allb.at[vec], to_sibling)
-    basis_copy.start()
 
     lane = lax.broadcasted_iota(jnp.int32, (rows, lanes), 1)
     row = lax.broadcasted_iota(jnp.int32, (rows, lanes), 0)
@@ -246,7 +245,7 @@
                 done.append(p)
             return tuple(done)
 
-        packed = lax.fori_loop(0, levels // 2, body, no_tiles, unroll=4)
+        packed = lax.fori_loop(0, levels // 2, body, no_tiles, unroll=8)
         for f in range(fields):
             lon_out[slot, f] = packed[f]
         pack_rows(tiles_ref, lat_out.at[slot])
@@ -270,8 +269,7 @@
                     ("slice", t, d, i), sel.at[t, pl.ds(i * piece, piece)], there, partner(d)
                 )
                 passes[t, d, i] = remote(("pass", t, d, i), there, there, to_sibling)
-                if t == 0:
-                    slices[t, d, i].start()
+                slices[t, d, i].start()
 
     spread(lambda where: allb[vec, where, :].astype(F32), field, 0)
     field_edges = [edge_copies("f", t, t) for t in range(STEPS)]
@@ -305,9 +303,6 @@
         for d, i in every:
             slices[t, d, i].wait_recv()
             passes[t, d, i].start()
-        if t + 1 < STEPS:
-            for d, i in every:
-                slices[t + 1, d, i].start()
 
     def build_state(t):
         for d, i in every:
@@ -349,7 +344,7 @@
                 moved[at(f, level), :] = tiles[f] - weight * change
             return carry
 
-        lax.fori_loop(0, levels, body, 0, unroll=4)
+        lax.fori_loop(0, levels, body, 0, unroll=8)
 
     def beyond(slot, f, level):
         place = pl.ds(f * levels + level, 1)
@@ -384,7 +379,7 @@
                 field[at(f, level), :] = done[f]
             return tuple(done)
 
-        lax.fori_loop(0, levels, forward, no_tiles, unroll=8)
+        lax.fori_loop(0, levels, forward, no_tiles, unroll=16)
         if t + 1 < STEPS:
             take_state(t + 1)
         last = t == STEPS - 1
@@ -403,7 +398,7 @@
                     edges.append(note_edges(level, x, packed[f]))
             return tuple(done), tuple(edges)
 
-        _, packed = lax.fori_loop(0, levels, backward, (no_tiles, () if last else no_tiles), unroll=8)
+        _, packed = lax.fori_loop(0, levels, backward, (no_tiles, () if last else no_tiles), unroll=16)
         if not last:
             for f in range(fields):
                 lon_out[t + 1, f] = packed[f]
@@ -418,6 +413,7 @@
             for d in range(1, pairs):
                 for f in range(1, fields):
                     cross[f, d].start()
+            basis_copy.start()
         interior(t)
         if t == STEPS - 1:
             relay_until(min(2, fields))
@@ -451,7 +447,7 @@
                 acc[i] += b[:rows] * low + b[rows:] * high
             return tuple(acc)
 
-        acc = lax.fori_loop(0, levels // 2, gram, acc, unroll=8)
+        acc = lax.fori_loop(0, levels // 2, gram, acc, unroll=12)
     part = jnp.zeros((8, lanes), F32)
     part_row = lax.broadcasted_iota(jnp.int32, (8, lanes), 0)
     for i in range(groups):
@@ -489,7 +485,7 @@
             field[at(f, 2 * m + 1), :] = high
             return carry
 
-        lax.fori_loop(0, levels // 2, residual, 0, unroll=8)
+        lax.fori_loop(0, levels // 2, residual, 0, unroll=12)
         chunk = pl.ds(f * per_field, per_field)
         copy = pltpu.make_async_copy(field.at[chunk], out_ref.at[chunk], local_sem.at[5 + f])
         copy.start()

time: 42.2 us -> 40.1 us (0.950)
  Pallas kernels: 41.4 us -> 39.2 us
    pallas_call x1, Pallas kernels: 39.3 us -> 37.2 us  [per_device(): pl.pallas_call(functools.partial(kernel, (fields, levels, rows, lanes), (...]
where the time goes in v7:
time: 40.1 us; the launch traced here: 39.9 us
  Pallas kernels  39.2 us (98%)
  between operations  0.64 us (2%)
    pallas_call x1, Pallas kernels, per_device(): pl.pallas_call(functools.partial(kernel, (fields, levels, rows, lanes), (...  37.2 us
    pallas_call x1, Pallas kernels, per_device(): pl.pallas_call(hand_over, out_shape=(jax.ShapeDtypeStruct((size, lanes),...  2.09 us

profile of v7, /device:TPU:0, one launch (start us, length us, event | category | flops | bytes accessed | tf_op | source)
XLA Modules:
  0.0 39.9 jit_solution(5008528940638066074)
XLA Ops:
  0.6 37.2 %shard_map.68 = (f32[1920,128]{1,0:T(8,128)}, f32[4,4]{1,0:T(4,128)}) custom-call(bf16[1920,128]{1,0:T(8,128)(2,1)} %bitcast.3, bf16[1920,128]{1,0:T(8,128)(2,1)} %bitcast.4, s32[4]{0:T(128)} %owner_in.1, f32[5,47]{1,0:T(8,128)} %diff_in.1, f32[5]{0:T(128)} %weight_in.1), custom_call_target="tpu_custom_call" | custom-call | tf_op jit(solution)/shard_map/pallas_call | solution.py:552
  37.8 2.1 %shard_map.69 = (f32[1920,128]{1,0:T(8,128)}, f32[4,4]{1,0:T(4,128)}) custom-call(f32[1920,128]{1,0:T(8,128)} %get-tuple-element.6.block_ref, f32[4,4]{1,0:T(4,128)} %get-tuple-element.7.coup_ref), custom_call_target="tpu_custom_call" | custom-call | tf_op jit(solution)/shard_map/pallas_call | solution.py:595

commit v8 on v7

--- a/solution.py
+++ b/solution.py
@@ -9,7 +9,7 @@
 from jax.sharding import PartitionSpec as P
 
 STEPS = 2
-PIECES = 2
+PIECES = 4
 CHUNKS = 4
 COURANT = 0.25
 MESH = pl.DeviceIdType.MESH
@@ -245,7 +245,7 @@
                 done.append(p)
             return tuple(done)
 
-        packed = lax.fori_loop(0, levels // 2, body, no_tiles, unroll=8)
+        packed = lax.fori_loop(0, levels // 2, body, no_tiles, unroll=12)
         for f in range(fields):
             lon_out[slot, f] = packed[f]
         pack_rows(tiles_ref, lat_out.at[slot])
@@ -344,7 +344,7 @@
                 moved[at(f, level), :] = tiles[f] - weight * change
             return carry
 
-        lax.fori_loop(0, levels, body, 0, unroll=8)
+        lax.fori_loop(0, levels, body, 0, unroll=12)
 
     def beyond(slot, f, level):
         place = pl.ds(f * levels + level, 1)
@@ -379,7 +379,7 @@
                 field[at(f, level), :] = done[f]
             return tuple(done)
 
-        lax.fori_loop(0, levels, forward, no_tiles, unroll=16)
+        lax.fori_loop(0, levels, forward, no_tiles, unroll=24)
         if t + 1 < STEPS:
             take_state(t + 1)
         last = t == STEPS - 1
@@ -398,7 +398,7 @@
                     edges.append(note_edges(level, x, packed[f]))
             return tuple(done), tuple(edges)
 
-        _, packed = lax.fori_loop(0, levels, backward, (no_tiles, () if last else no_tiles), unroll=16)
+        _, packed = lax.fori_loop(0, levels, backward, (no_tiles, () if last else no_tiles), unroll=24)
         if not last:
             for f in range(fields):
                 lon_out[t + 1, f] = packed[f]
@@ -447,7 +447,7 @@
                 acc[i] += b[:rows] * low + b[rows:] * high
             return tuple(acc)
 
-        acc = lax.fori_loop(0, levels // 2, gram, acc, unroll=12)
+        acc = lax.fori_loop(0, levels // 2, gram, acc, unroll=24)
     part = jnp.zeros((8, lanes), F32)
     part_row = lax.broadcasted_iota(jnp.int32, (8, lanes), 0)
     for i in range(groups):
@@ -485,7 +485,7 @@
             field[at(f, 2 * m + 1), :] = high
             return carry
 
-        lax.fori_loop(0, levels // 2, residual, 0, unroll=12)
+        lax.fori_loop(0, levels // 2, residual, 0, unroll=24)
         chunk = pl.ds(f * per_field, per_field)
         copy = pltpu.make_async_copy(field.at[chunk], out_ref.at[chunk], local_sem.at[5 + f])
         copy.start()

time: 40.1 us -> 40.2 us (level)
  no operation moved by 1% of the time
where the time goes in v8:
time: 40.2 us; the launch traced here: 40 us
  Pallas kernels  39.4 us (98%)
  between operations  0.64 us (2%)
    pallas_call x1, Pallas kernels, per_device(): pl.pallas_call(functools.partial(kernel, (fields, levels, rows, lanes), (...  37.3 us
    pallas_call x1, Pallas kernels, per_device(): pl.pallas_call(hand_over, out_shape=(jax.ShapeDtypeStruct((size, lanes),...  2.09 us

profile of v8, /device:TPU:0, one launch (start us, length us, event | category | flops | bytes accessed | tf_op | source)
XLA Modules:
  0.0 40.0 jit_solution(8031510320289904410)
XLA Ops:
  0.6 37.3 %shard_map.68 = (f32[1920,128]{1,0:T(8,128)}, f32[4,4]{1,0:T(4,128)}) custom-call(bf16[1920,128]{1,0:T(8,128)(2,1)} %bitcast.3, bf16[1920,128]{1,0:T(8,128)(2,1)} %bitcast.4, s32[4]{0:T(128)} %owner_in.1, f32[5,47]{1,0:T(8,128)} %diff_in.1, f32[5]{0:T(128)} %weight_in.1), custom_call_target="tpu_custom_call" | custom-call | tf_op jit(solution)/shard_map/pallas_call | solution.py:552
  37.9 2.1 %shard_map.69 = (f32[1920,128]{1,0:T(8,128)}, f32[4,4]{1,0:T(4,128)}) custom-call(f32[1920,128]{1,0:T(8,128)} %get-tuple-element.6.block_ref, f32[4,4]{1,0:T(4,128)} %get-tuple-element.7.coup_ref), custom_call_target="tpu_custom_call" | custom-call | tf_op jit(solution)/shard_map/pallas_call | solution.py:595

commit v9 on v7

--- a/solution.py
+++ b/solution.py
@@ -41,6 +41,7 @@
     diff_in,
     weight_in,
     out_ref,
+    coup_out,
     coup_ref,
     owner_ref,
     diff_ref,
@@ -499,8 +500,9 @@
         table = jnp.where(wide_lane == j, cols[j], table)
     coup_ref[...] = table[:groups, :groups]
 
-    for copy in out_copies:
-        copy.wait()
+    coup_copy = pltpu.make_async_copy(coup_ref, coup_out, local_sem.at[5 + fields])
+    coup_copy.start()
+    out_copies.append(coup_copy)
     for copy in traj_copies:
         copy.wait_send()
     basis_copy.wait_send()
@@ -517,6 +519,8 @@
         await_edges_sent(state_edges[t])
     for copy in sum_copies + col_copies:
         copy.wait_send()
+    for copy in out_copies:
+        copy.wait()
 
 
 def hand_over(block_ref, coup_ref, block_out, coup_out, block, coup, in_sem, out_sem):
@@ -547,7 +551,6 @@
         pairs, tiles = groups // 2, lats * lons
         ids = copy_names(pairs, tiles, groups, fields)
         slots = 2 * STEPS
-        vmem = pl.BlockSpec(memory_space=pltpu.VMEM)
         hbm = pl.BlockSpec(memory_space=pltpu.HBM)
         residual_block, coupling = pl.pallas_call(
             functools.partial(kernel, (fields, levels, rows, lanes), (groups, lats, lons), ids),
@@ -556,8 +559,9 @@
                 jax.ShapeDtypeStruct((groups, groups), F32),
             ),
             in_specs=[hbm] * 5,
-            out_specs=(hbm, vmem),
+            out_specs=(hbm, hbm),
             scratch_shapes=[
+                pltpu.VMEM((groups, groups), F32),
                 pltpu.SMEM(slice_owner.shape, jnp.int32),
                 pltpu.SMEM(diffusion.shape, F32),
                 pltpu.SMEM(energy_weight.shape, F32),
@@ -578,7 +582,7 @@
                 pltpu.VMEM((slots, 2, fields * levels, lanes), F32),
                 pltpu.VMEM((tiles, 8, lanes), F32),
                 pltpu.VMEM((groups, 8, lanes), F32),
-                pltpu.SemaphoreType.DMA((5 + fields,)),
+                pltpu.SemaphoreType.DMA((6 + fields,)),
                 pltpu.SemaphoreType.DMA((len(ids),)),
                 pltpu.SemaphoreType.DMA((len(ids),)),
             ],

time: 40.1 us -> 40 us (level)
  no operation moved by 1% of the time
where the time goes in v9:
time: 40 us; the launch traced here: 39.8 us
  Pallas kernels  39.2 us (98%)
  between operations  0.64 us (2%)
    pallas_call x1, Pallas kernels, per_device(): pl.pallas_call(functools.partial(kernel, (fields, levels, rows, lanes), (...  37.1 us
    pallas_call x1, Pallas kernels, per_device(): pl.pallas_call(hand_over, out_shape=(jax.ShapeDtypeStruct((size, lanes),...  2.09 us

profile of v9, /device:TPU:0, one launch (start us, length us, event | category | flops | bytes accessed | tf_op | source)
XLA Modules:
  0.0 39.8 jit_solution(6250341062492240870)
XLA Ops:
  0.6 37.1 %shard_map.68 = (f32[1920,128]{1,0:T(8,128)}, f32[4,4]{1,0:T(4,128)}) custom-call(bf16[1920,128]{1,0:T(8,128)(2,1)} %bitcast.3, bf16[1920,128]{1,0:T(8,128)(2,1)} %bitcast.4, s32[4]{0:T(128)} %owner_in.1, f32[5,47]{1,0:T(8,128)} %diff_in.1, f32[5]{0:T(128)} %weight_in.1), custom_call_target="tpu_custom_call" | custom-call | tf_op jit(solution)/shard_map/pallas_call | solution.py:555
  37.7 2.1 %shard_map.69 = (f32[1920,128]{1,0:T(8,128)}, f32[4,4]{1,0:T(4,128)}) custom-call(f32[1920,128]{1,0:T(8,128)} %get-tuple-element.6.block_ref, f32[4,4]{1,0:T(4,128)} %get-tuple-element.7.coup_ref), custom_call_target="tpu_custom_call" | custom-call | tf_op jit(solution)/shard_map/pallas_call | solution.py:599
